TPU v7x, 512 devices: a whole 4x4x16 slice. The times are simulated.
512 devices in a mesh: grp: 16 (over y_hi, x, core), dev: 32 (over y_lo, z).
Axes of the slice: x: 4, y: 4 (y_hi: 2, y_lo: 2; y = y_hi * 2 + y_lo), z: 16, core: 2. Of those that a mesh axis runs over, the one named last changes fastest.
Arguments:
- ctx_hidden: bfloat16 [2048, 3584], P('dev'), may hold values from -410 to 410
- step_hidden: bfloat16 [1536, 64, 3584], P(('grp', 'dev')), may hold values from -410 to 410
- norm_gain: float32 [3584], replicated, may hold values from 0.1 to 1.9
- w_query: bfloat16 [3584, 1792], P('dev'), may hold values from -4 to 4
- w_keyval: bfloat16 [3584, 512], P('dev'), may hold values from -24 to 24
- step_lengths: int32 [1536], P(('grp', 'dev')), may hold values from 1 to 64, as said below
- step_mask: int32 [1536, 64, 64], P(('grp', 'dev')), may hold values 0 or 1
Outputs:
- attn_out: bfloat16 [1536, 64, 1792], P(('grp', 'dev'))
Inputs may be any that keep to these rules, and one draw needn't show every extreme that they name: `step_lengths`: each step's live tokens stand at its front; some solution fills all 64 slots.
All inputs are finite; a program needn't handle non-finite values. No bound on the sum of `step_mask` on one device may be relied on, other than what follows from the above.
Results may differ from a plain program's by a relative error of at most 0.009.
The roundings to bfloat16 on the way count: a program that leaves them out, or rounds other values in their place, can miss the bound.
Values may be sent and summed in bfloat16 or wider, within the bound.
No kernel may reach another device: no remote copies, remote signals or barrier semaphores. Data moves between devices by JAX's collectives and lax.ppermute only.
A program may use at most 128 MiB of HBM per device.

v0:
```python
import math

import jax
import jax.numpy as jnp
from jax import lax
from jax.sharding import PartitionSpec as P

HEAD_SIZE = 128


NEG_FILL = -1e30


def rms_norm(hidden_rows, norm_gain):
    widened = hidden_rows.astype(jnp.float32)
    inverse = lax.rsqrt(jnp.mean(widened * widened, axis=-1, keepdims=True) + 1e-06)
    return (widened * inverse * norm_gain).astype(jnp.bfloat16)


def projector(source, incoming):
    return jnp.dot(source, incoming, preferred_element_type=jnp.float32)


def local(ctx_hidden, step_hidden, norm_gain, w_query, w_keyval, step_lengths, step_mask):
    samples, step_count, features = step_hidden.shape
    row_count = samples * step_count
    kv_cols = w_keyval.shape[1]
    key_cols = kv_cols // 2
    kv_heads = key_cols // HEAD_SIZE
    query_cols = w_query.shape[1]
    head_groups = query_cols // HEAD_SIZE // kv_heads
    score_scale = 1.0 / math.sqrt(HEAD_SIZE)
    share_rows = ctx_hidden.shape[0] // lax.axis_size("grp")
    own_context = lax.dynamic_slice_in_dim(
        ctx_hidden, lax.axis_index("grp") * share_rows, share_rows, 0
    )
    own_count = own_context.shape[0]
    normed_context = rms_norm(own_context, norm_gain)
    normed_step = rms_norm(step_hidden.reshape(row_count, features), norm_gain)
    both_rows = jnp.concatenate([normed_context, normed_step], 0)
    keyval = projector(both_rows, lax.all_gather(w_keyval, "dev", axis=0, tiled=True))
    keyval = keyval.astype(jnp.bfloat16)
    problem_keyval = keyval[:own_count]
    solution_keyval = keyval[own_count:]
    query_block = projector(normed_step, lax.all_gather(w_query, "dev", axis=0, tiled=True))
    query_block = query_block.astype(jnp.bfloat16)
    query_rows = query_block.reshape(row_count, kv_heads, head_groups, HEAD_SIZE)
    context_keys = problem_keyval[:, :key_cols]
    context_values = problem_keyval[:, key_cols:]
    context_keys, context_values = (
        lax.all_gather(context_keys, "grp", axis=0, tiled=True),
        lax.all_gather(context_values, "grp", axis=0, tiled=True),
    )
    row_top = jnp.full((row_count, kv_heads, head_groups), NEG_FILL, jnp.float32)
    key_rows = lax.all_gather(context_keys, "dev", axis=0, tiled=True).reshape(
        -1, kv_heads, HEAD_SIZE
    )
    value_rows = lax.all_gather(context_values, "dev", axis=0, tiled=True).reshape(
        -1, kv_heads, HEAD_SIZE
    )
    scores = (
        jnp.einsum("rhgd,nhd->rhgn", query_rows, key_rows, preferred_element_type=jnp.float32)
        * score_scale
    )
    new_top = jnp.maximum(row_top, scores.max(-1))
    weights = jnp.exp(scores - new_top[..., None])
    weight_sum = weights.sum(-1)
    accumulated = jnp.einsum(
        "rhgn,nhd->rhgd",
        weights.astype(jnp.bfloat16),
        value_rows,
        preferred_element_type=jnp.float32,
    )
    running = (new_top, weight_sum, accumulated)
    row_top, weight_sum, accumulated = running
    row_top = row_top.reshape(samples, step_count, kv_heads, head_groups)
    weight_sum = weight_sum.reshape(samples, step_count, kv_heads, head_groups)
    accumulated = accumulated.reshape(samples, step_count, kv_heads, head_groups, HEAD_SIZE)
    step_keys = solution_keyval[:, :key_cols].reshape(samples, step_count, kv_heads, HEAD_SIZE)
    step_values = solution_keyval[:, key_cols:].reshape(samples, step_count, kv_heads, HEAD_SIZE)
    step_queries = query_block.reshape(samples, step_count, kv_heads, head_groups, HEAD_SIZE)
    scores = (
        jnp.einsum("sthgd,suhd->sthgu", step_queries, step_keys, preferred_element_type=jnp.float32)
        * score_scale
    )
    positions = lax.iota(jnp.int32, step_count)
    causal = positions[None, :] <= positions[:, None]
    diagonal = positions[None, :] == positions[:, None]
    allowed = (
        causal[None]
        & (diagonal[None] | (step_mask == 1))
        & (positions[None, None, :] < step_lengths[:, None, None])
    )
    scores = jnp.where(allowed[:, :, None, None, :], scores, NEG_FILL)
    new_top = jnp.maximum(row_top, scores.max(-1))
    shrink = jnp.exp(row_top - new_top)
    weights = jnp.exp(scores - new_top[..., None])
    weight_sum = weight_sum * shrink + weights.sum(-1)
    accumulated = accumulated * shrink[..., None] + jnp.einsum(
        "sthgu,suhd->sthgd",
        weights.astype(jnp.bfloat16),
        step_values,
        preferred_element_type=jnp.float32,
    )
    attended = accumulated / weight_sum[..., None]
    live_rows = positions[None, :] < step_lengths[:, None]
    attended = jnp.where(live_rows[:, :, None, None, None], attended, 0.0)
    return attended.reshape(samples, step_count, query_cols).astype(jnp.bfloat16)


def solution(mesh):
    placed = (
        P("dev", None),
        P(("grp", "dev"), None, None),
        P(),
        P("dev", None),
        P("dev", None),
        P(("grp", "dev")),
        P(("grp", "dev"), None, None),
    )
    return jax.shard_map(
        local, mesh=mesh, in_specs=placed, out_specs=P(("grp", "dev"), None, None), check_vma=False
    )
```

profile of v0, /device:TPU:1, one launch (start us, length us, event | category | flops | bytes accessed | tf_op | source)
XLA Modules:
  0.0 627.9 jit_solution(1606231819222027045)
XLA Ops:
  6.5 0.0 all-gather.7.cloned.1.call-start
  6.5 0.7 all-gather.7.cloned.1.call-update
  7.3 0.0 all-gather.9.cloned.1.call-start
  7.3 1.7 multiply_reduce_fusion
  9.0 0.1 rsqrt.21
  9.1 1.0 fusion.29
  10.1 0.0 copy-done.5
  10.1 0.9 fusion.31
  11.0 0.0 copy-done
  11.0 0.4 fusion.6
  11.4 0.0 copy-start.6
  11.4 0.0 copy-start.3
  11.4 122.5 %all-gather.7.cloned.1.call-done = bf16[3584,512]{1,0:T(8,128)(2,1)} async-done(((bf16[112,512]{1,0:T(8,128)(2,1)}), bf16[3584,512]{1,0:T(8,128)(2,1)}) %all-gather.7.cloned.1.call-update) | async-done | bytes 3670032 | tf_op jit(solution)/shard_map/all_gather | solution.py:41
  133.9 2.9 fusion.19
  136.9 42.4 %all-gather = bf16[16,4,256]{2,1,0:T(4,128)(2,1)S(1)} all-gather(bf16[1,4,256]{2,1,0:T(4,128)(2,1)S(1)} %get-tuple-element.10), channel_id=1, replica_groups=mesh['grp'=16,'dev'=32] {'grp'}, dimensions={0}, use_global_device_ids=true | all-gather | bytes 34816 | tf_op jit(solution)/shard_map/all_gather | solution.py:52
  179.3 0.6 reshape.167
  179.9 0.0 all-gather.9.cloned.1.call-update
  179.9 0.0 all-gather.11.cloned.1.call-start
  180.0 19.3 %all-gather.1 = bf16[16,4,256]{2,1,0:T(4,128)(2,1)S(1)} all-gather(bf16[1,4,256]{2,1,0:T(4,128)(2,1)S(1)} %get-tuple-element.9), channel_id=1, replica_groups=mesh['grp'=16,'dev'=32] {'grp'}, dimensions={0}, use_global_device_ids=true | all-gather | bytes 34816 | tf_op jit(solution)/shard_map/all_gather | solution.py:51
  199.3 0.6 reshape.169
  199.9 0.0 all-gather.11.cloned.1.call-update
  200.0 0.2 all-gather.13.cloned.1.call-start
  200.2 0.3 all-gather.13.cloned.1.call-update
  200.6 0.0 copy-done.6
  200.6 0.1 iota_compare_fusion.2
  200.7 0.0 copy-done.3
  200.7 0.1 copy.39
  200.9 0.7 reshape.161
  201.5 0.7 reshape.163
  202.2 76.6 %all-gather.9.cloned.1.call-done = bf16[2048,256]{1,0:T(8,128)(2,1)} async-done(((bf16[64,256]{1,0:T(8,128)(2,1)}), bf16[2048,256]{1,0:T(8,128)(2,1)}) %all-gather.9.cloned.1.call-update) | async-done | bytes 1048592 | tf_op jit(solution)/shard_map/all_gather | solution.py:58
  278.8 1.5 copy.33
  280.2 125.3 %all-gather.11.cloned.1.call-done = bf16[2048,256]{1,0:T(8,128)(2,1)} async-done(((bf16[64,256]{1,0:T(8,128)(2,1)}), bf16[2048,256]{1,0:T(8,128)(2,1)}) %all-gather.11.cloned.1.call-update) | async-done | bytes 1048592 | tf_op jit(solution)/shard_map/all_gather | solution.py:55
  405.6 1.5 copy.34
  407.1 170.6 %all-gather.13.cloned.1.call-done = bf16[3584,1792]{1,0:T(8,128)(2,1)} async-done(((bf16[112,1792]{1,0:T(8,128)(2,1)}), bf16[3584,1792]{1,0:T(8,128)(2,1)}) %all-gather.13.cloned.1.call-update) | async-done | bytes 12845072 | tf_op jit(solution)/shard_map/all_gather | solution.py:45
  577.7 8.2 %convolution_convert_fusion = bf16[192,1792]{1,0:T(8,128)(2,1)} fusion(bf16[192,3584]{1,0:T(8,128)(2,1)S(1)} %fusion.6, bf16[3584,1792]{1,0:T(8,128)(2,1)} %all-gather.13.cloned.1.call-done), kind=kOutput, calls=%fused_computation.10 | convolution fusion | flops 2466594816 | bytes 14909440 | tf_op jit(solution)/shard_map/dot_general | solution.py:21
  585.8 1.9 reshape.159
  587.7 2.6 reshape.162
  590.3 8.9 %bitcast_reduce_fusion = (f32[192,2,7]{0,2,1:T(8,128)S(1)}, f32[2,2048,192,7]{1,2,3,0:T(8,128)}) fusion(bf16[2048,2,128,1]{0,2,3,1:T(8,128)(2,1)S(1)} %bitcast.59, bf16[192,2,7,128]{3,2,1,0:T(8,128)(2,1)S(1)} %reshape.159), kind=kOutput, calls=%fused_computation.1 | convolution fusion | flops 1420293504 | bytes 23767552 | tf_op jit(solution)/shard_map/rhgd,nhd->rhgn/dot_general | solution.py:62
  599.2 0.1 reshape.175
  599.3 8.3 %fusion.1 = f32[192,2,7]{0,2,1:T(8,128)S(1)} fusion(f32[2,2048,192,7]{1,2,3,0:T(8,128)} %get-tuple-element.12, f32[192,2,7]{0,2,1:T(8,128)S(1)} %broadcast_maximum_fusion), kind=kLoop, calls=%fused_computation.3 | loop fusion | flops 16512384 | bytes 22041600 | tf_op jit(solution)/shard_map/reduce_sum | solution.py:67
  607.6 0.0 copy-start.1
  607.6 9.3 %fusion.3 = f32[2,128,192,7]{1,2,3,0:T(8,128)S(1)} fusion(bf16[2048,2,128,1]{0,2,3,1:T(8,128)(2,1)S(1)} %bitcast.58, f32[2,2048,192,7]{1,2,3,0:T(8,128)} %get-tuple-element.12, f32[192,2,7]{0,2,1:T(8,128)S(1)} %broadcast_maximum_fusion), kind=kOutput, calls=%fused_computation.5 | convolution fusion | flops 1425801216 | bytes 24455680 | tf_op jit(solution)/shard_map/rhgn,nhd->rhgd/dot_general | solution.py:68
  616.9 0.1 reshape.174
  617.0 0.7 fusion.36
  617.7 0.3 fusion.17
  618.1 1.3 fusion.16
  619.4 0.5 copy.49
  619.8 1.6 convert_element_type.47
  (16 shorter events, 0.2 us)
Async XLA Ops:
  6.5 4.5 copy-start
  6.5 3.5 copy-start.5
  6.5 127.4 %all-gather.7.cloned.1.call-start = ((), (), s32[]{:S(2)}) async-start(), calls=%async_computation | async-start | bytes 3784704 | tf_op jit(solution)/shard_map/all_gather | solution.py:41
  7.3 271.5 %all-gather.9.cloned.1.call-start = ((), (), s32[]{:S(2)}) async-start(), calls=%async_computation.1 | async-start | bytes 1081344 | tf_op jit(solution)/shard_map/all_gather | solution.py:58
  11.4 189.2 %copy-start.6 = (s32[3]{0:T(128)S(1)}, s32[3]{0:T(128)}, u32[]{:S(2)}) copy-start(s32[3]{0:T(128)} %param.12) | copy-start | bytes 40
  11.4 189.2 %copy-start.3 = (s32[3,64,64]{2,1,0:T(8,128)S(1)}, s32[3,64,64]{2,1,0:T(8,128)}, u32[]{:S(2)}) copy-start(s32[3,64,64]{2,1,0:T(8,128)} %param.13) | copy-start | bytes 147460
  179.9 225.6 %all-gather.11.cloned.1.call-start = ((), (), s32[]{:S(2)}) async-start(), calls=%async_computation.2 | async-start | bytes 1081344 | tf_op jit(solution)/shard_map/all_gather | solution.py:55
  200.0 377.7 %all-gather.13.cloned.1.call-start = ((), (), s32[]{:S(2)}) async-start(), calls=%async_computation.3 | async-start | bytes 13246464 | tf_op jit(solution)/shard_map/all_gather | solution.py:45
  607.6 9.4 %copy-start.1 = (bf16[3,64,2,7,128]{4,3,2,1,0:T(8,128)(2,1)S(1)}, bf16[3,64,2,7,128]{4,3,2,1,0:T(8,128)(2,1)}, u32[]{:S(2)}) copy-start(bf16[3,64,2,7,128]{4,3,2,1,0:T(8,128)(2,1)} %reshape.162) | copy-start | bytes 2064388
  607.6 9.4 %copy-start.2 = (bf16[3,64,2,128]{3,2,1,0:T(2,128)(2,1)S(1)}, bf16[3,64,2,128]{3,2,1,0:T(2,128)(2,1)}, u32[]{:S(2)}) copy-start(bf16[3,64,2,128]{3,2,1,0:T(2,128)(2,1)} %reshape.161) | copy-start | bytes 294916
  617.0 1.1 copy-start.4
Sparse Core Ops, SparseCore 0:
  9.4 124.4 all-gather.6
  180.1 98.6 all-gather.8
  280.8 124.7 all-gather.10
  407.5 170.1 all-gather.12
where the time goes:
time: 632 us; the launch traced here: 628 us
  waiting for transfers between devices  496 us (78%)
  blocking collectives  61.8 us (10%)
  matrix products  31.2 us (5%)
  between operations  13.3 us (2%)
  other arithmetic  12.8 us (2%)
  local copies, waits for them, and re-layouts  12.5 us (2%)
    all_gather x1, waiting for transfers between devices, local(): lax.all_gather(w_query, 'dev', axis=0, tiled=True)  171 us
    all_gather x1, waiting for transfers between devices, local(): lax.all_gather(context_keys, 'dev', axis=0, tiled=True)  125 us
    all_gather x1, waiting for transfers between devices, local(): lax.all_gather(w_keyval, 'dev', axis=0, tiled=True)  122 us
    all_gather x1, waiting for transfers between devices, local(): lax.all_gather(context_values, 'dev', axis=0, tiled=True)  76.6 us
    all_gather x1, blocking collectives, local(): lax.all_gather(context_values, 'grp', axis=0, tiled=True)  42.4 us
    all_gather x1, blocking collectives, local(): lax.all_gather(context_keys, 'grp', axis=0, tiled=True)  19.3 us
  transfers between devices with their start and end apart: 4, of which 4 were waited for; matrix products, arithmetic and copies ran while one was open for 1% of the time, Pallas kernels for 0%

commit v1 on v0

v1 whole, which is shorter than its diff:
```python
import functools
import math

import jax
import jax.numpy as jnp
from jax import lax
from jax.experimental import pallas as pl
from jax.experimental.pallas import tpu as pltpu
from jax.sharding import Mesh
from jax.sharding import PartitionSpec as P

HEAD_SIZE = 128
NEG_FILL = -1e30
AXES = ("yh", "x", "core", "yl", "z")
SWAP = [(0, 1), (1, 0)]


def rms_norm(hidden_rows, norm_gain):
    widened = hidden_rows.astype(jnp.float32)
    inverse = lax.rsqrt(jnp.mean(widened * widened, axis=-1, keepdims=True) + 1e-06)
    return (widened * inverse * norm_gain).astype(jnp.bfloat16)


def dot(a, b):
    return jnp.dot(a, b, preferred_element_type=jnp.float32)


def spread(block, axis):
    size = lax.axis_size(axis)
    return lax.all_to_all(jnp.broadcast_to(block[None], (size,) + block.shape), axis, 0, 0, tiled=True)


def attend_kernel(heads, query, keys, values, step_keys, step_values, allowed, out):
    slots = query.shape[0]
    scale = math.log2(math.e) / math.sqrt(HEAD_SIZE)
    rows = jnp.concatenate([query[:, h * HEAD_SIZE : (h + 1) * HEAD_SIZE] for h in range(heads)], 0)
    contract = (((1,), (1,)), ((), ()))
    far = lax.dot_general(rows, keys[...], contract, preferred_element_type=jnp.float32)
    near = lax.dot_general(rows, step_keys[...], contract, preferred_element_type=jnp.float32)
    seen = jnp.concatenate([allowed[...][:, :slots].astype(jnp.float32)] * heads, 0) > 0.5
    near = jnp.where(seen, near, NEG_FILL)
    top = jnp.maximum(far.max(-1, keepdims=True), near.max(-1, keepdims=True))
    far_weights = jnp.exp2((far - top) * scale)
    near_weights = jnp.exp2((near - top) * scale)
    total = far_weights.sum(-1, keepdims=True) + near_weights.sum(-1, keepdims=True)
    attended = dot(far_weights.astype(jnp.bfloat16), values[...])
    attended = attended + dot(near_weights.astype(jnp.bfloat16), step_values[...])
    attended = (attended / total).astype(jnp.bfloat16)
    out[...] = jnp.concatenate([attended[h * slots : (h + 1) * slots] for h in range(heads)], 1)


def attend(query, keys, values, step_keyval, allowed, slots):
    rows, cols = query.shape
    heads = cols // HEAD_SIZE
    tokens = keys.shape[0]
    whole = pl.BlockSpec((tokens, HEAD_SIZE), lambda i: (0, 0))
    return pl.pallas_call(
        functools.partial(attend_kernel, heads),
        grid=(rows // slots,),
        in_specs=[
            pl.BlockSpec((slots, cols), lambda i: (i, 0)),
            whole,
            whole,
            pl.BlockSpec((slots, HEAD_SIZE), lambda i: (i, 0)),
            pl.BlockSpec((slots, HEAD_SIZE), lambda i: (i, 1)),
            pl.BlockSpec((slots, allowed.shape[1]), lambda i: (i, 0)),
        ],
        out_specs=pl.BlockSpec((slots, cols), lambda i: (i, 0)),
        out_shape=jax.ShapeDtypeStruct((rows, cols), jnp.bfloat16),
        compiler_params=pltpu.CompilerParams(vmem_limit_bytes=40 * 2**20),
        cost_estimate=pl.CostEstimate(
            flops=4 * rows * cols * tokens, bytes_accessed=4 * rows * cols, transcendentals=rows * heads * tokens
        ),
    )(query, keys, values, step_keyval, step_keyval, allowed)


def local(ctx_hidden, step_hidden, norm_gain, w_query, w_keyval, step_lengths, step_mask):
    samples, slots, features = step_hidden.shape
    rows = samples * slots
    kv_heads = w_keyval.shape[1] // (2 * HEAD_SIZE)
    cols = w_query.shape[1] // kv_heads
    share = w_query.shape[0]
    core, x = lax.axis_index("core"), lax.axis_index("x")

    own_query = lax.dynamic_slice_in_dim(w_query, core * cols, cols, 1)
    pair_query = lax.all_gather(own_query, "yl", axis=0, tiled=True)
    full_query = lax.all_gather(pair_query, "z", axis=0, tiled=True)

    own_kv = lax.dynamic_slice_in_dim(w_keyval, ((x % 2) * kv_heads + core) * HEAD_SIZE, HEAD_SIZE, 1)
    pair_kv = lax.all_gather(own_kv, "yl", axis=0, tiled=True)
    half_kv = spread(pair_kv, "z").reshape(features, HEAD_SIZE)
    other_kv = lax.ppermute(half_kv, "x", [(i, i ^ 1) for i in range(lax.axis_size("x"))])

    def reorder(normed):
        count = normed.shape[0]
        return normed.reshape(count, 2, features // share // 2, share).swapaxes(1, 2).reshape(count, features)

    token_share = ctx_hidden.shape[0] // 2
    own_context = lax.dynamic_slice_in_dim(ctx_hidden, (x // 2) * token_share, token_share, 0)
    normed_context = reorder(rms_norm(own_context, norm_gain))
    context_block = dot(normed_context, half_kv).astype(jnp.bfloat16)
    context_block = lax.all_gather(context_block, "yl", axis=0, tiled=True)
    context_block = spread(context_block, "z").reshape(-1, HEAD_SIZE)
    context_all = spread(context_block, "x")
    keys = jnp.concatenate([context_all[0], context_all[2]], 0)
    values = jnp.concatenate([context_all[1], context_all[3]], 0)

    positions = lax.iota(jnp.int32, slots)
    causal = positions[None, :] <= positions[:, None]
    diagonal = positions[None, :] == positions[:, None]
    allowed = (
        causal[None]
        & (diagonal[None] | (step_mask == 1))
        & (positions[None, None, :] < step_lengths[:, None, None])
    )
    allowed = jnp.pad(allowed.astype(jnp.bfloat16).reshape(rows, slots), ((0, 0), (0, HEAD_SIZE - slots)))
    normed_step = reorder(rms_norm(step_hidden.reshape(rows, features), norm_gain))
    own_rows = jnp.concatenate([normed_step, allowed], 1)
    both_rows = jnp.concatenate([own_rows, lax.ppermute(own_rows, "core", SWAP)], 0)
    normed_rows, allowed_rows = both_rows[:, :features], both_rows[:, features:]

    is_key = x % 2 == 0
    keyval_weights = jnp.concatenate(
        [jnp.where(is_key, half_kv, other_kv), jnp.where(is_key, other_kv, half_kv)], 1
    )
    step_keyval = dot(normed_rows, keyval_weights).astype(jnp.bfloat16)
    query = dot(normed_rows, full_query).astype(jnp.bfloat16)
    attended = attend(query, keys, values, step_keyval, allowed_rows, slots)

    mine, theirs = attended[:rows], lax.ppermute(attended[rows:], "core", SWAP)
    first = core == 0
    result = jnp.concatenate([jnp.where(first, mine, theirs), jnp.where(first, theirs, mine)], 1)
    result = result.reshape(samples, slots, kv_heads * cols)
    live_rows = positions[None, :] < step_lengths[:, None]
    return jnp.where(live_rows[:, :, None], result, jnp.bfloat16(0.0))


def solution(mesh):
    five = Mesh(mesh.devices.reshape(2, 4, 2, 2, 16), AXES)
    dev, everywhere = ("yl", "z"), AXES
    placed = (
        P(dev, None),
        P(everywhere, None, None),
        P(),
        P(dev, None),
        P(dev, None),
        P(everywhere),
        P(everywhere, None, None),
    )
    return jax.shard_map(
        local, mesh=five, in_specs=placed, out_specs=P(everywhere, None, None), check_vma=False
    )
```

time: 632 us -> 191 us (0.30)
  waiting for transfers between devices: 496 us -> 60.8 us
  blocking collectives: 61.8 us -> 13 us
  starting transfers between devices: 0.3 us -> 46.8 us
  matrix products: 31.2 us -> 8.96 us
  Pallas kernels: 0 us -> 15.1 us
    all_gather x4 -> x1, waiting for transfers between devices: 495 us -> 19.8 us  [local(): full_query = lax.all_gather(pair_query, 'z', axis=0, tiled=True)]
    all_gather x2 -> x3, blocking collectives: 61.8 us -> 13 us  [the longest x1 5.99 us: local(): pair_query = lax.all_gather(own_query, 'yl', axis=0, tiled=True)]
    all_to_all x0 -> x3, waiting for transfers between devices: none -> 39.7 us  [spread(): lax.all_to_all(jnp.broadcast_to(block[None], (size,) + block.shape), axis...]
    all_to_all x0 -> x3, starting transfers between devices: none -> 33.9 us  [spread(): lax.all_to_all(jnp.broadcast_to(block[None], (size,) + block.shape), axis...]
    dot_general x6 -> x3, matrix products: 31.2 us -> 8.96 us  [dot(): return jnp.dot(a, b, preferred_element_type=jnp.float32)]
    pallas_call x0 -> x1, Pallas kernels: none -> 15.1 us  [attend(): pl.pallas_call(functools.partial(attend_kernel, heads), grid=(rows // slo...]
    ppermute x0 -> x3, starting transfers between devices: none -> 12.8 us  [the longest x1 4.94 us: local(): lax.ppermute(own_rows, 'core', SWAP)]
    reduce_sum x2 -> x0, other arithmetic: 8.63 us -> none  [the longest x1 8.31 us: local(): weight_sum = weights.sum(-1)]
  transfers between devices with their start and end apart: 4 -> 7, of which waited for: 4 -> 5; matrix products, arithmetic and copies ran while one was open for 1% -> 16% of each run, Pallas kernels for 0% -> 0%
where the time goes in v1:
time: 191 us; the launch traced here: 190 us
  waiting for transfers between devices  60.8 us (32%)
  starting transfers between devices  46.8 us (25%)
  local copies, waits for them, and re-layouts  18.5 us (10%)
  Pallas kernels  15.1 us (8%)
  between operations  13.7 us (7%)
  blocking collectives  13 us (7%)
  other arithmetic  12.8 us (7%)
  matrix products  8.96 us (5%)
    all_to_all x3, waiting for transfers between devices, spread(): lax.all_to_all(jnp.broadcast_to(block[None], (size,) + block.shape), axis...  39.7 us
    all_to_all x3, starting transfers between devices, spread(): lax.all_to_all(jnp.broadcast_to(block[None], (size,) + block.shape), axis...  33.9 us
    all_gather x1, waiting for transfers between devices, local(): full_query = lax.all_gather(pair_query, 'z', axis=0, tiled=True)  19.8 us
    pallas_call x1, Pallas kernels, attend(): pl.pallas_call(functools.partial(attend_kernel, heads), grid=(rows // slo...  15.1 us
    dot_general x3, matrix products, dot(): return jnp.dot(a, b, preferred_element_type=jnp.float32)  8.96 us
    reshape x4, local copies, waits for them, and re-layouts, reorder(): normed.reshape(count, 2, features // share // 2, share).swapaxes(1, 2)  6.67 us
    all_gather x1, blocking collectives, local(): pair_query = lax.all_gather(own_query, 'yl', axis=0, tiled=True)  5.99 us
    ppermute x1, starting transfers between devices, local(): lax.ppermute(own_rows, 'core', SWAP)  4.94 us
  transfers between devices with their start and end apart: 7, of which 5 were waited for; matrix products, arithmetic and copies ran while one was open for 16% of the time, Pallas kernels for 0%

profile of v1, /device:TPU:1, one launch (start us, length us, event | category | flops | bytes accessed | tf_op | source)
XLA Modules:
  0.0 189.7 jit_solution(568039734339083939)
XLA Ops:
  6.5 1.0 copy-done
  7.6 6.0 %all_gather.12 = bf16[224,896]{1,0:T(8,128)(2,1)} all-gather(bf16[112,896]{1,0:T(8,128)(2,1)S(1)} %constant_dynamic-slice_fusion.1), channel_id=1, replica_groups=mesh['yh'=2,'x'=4,'core'=2,'yl'=2,'z'=16] {'yl'}, dimensions={0}, use_global_device_ids=true | all-gather | bytes 602112 | tf_op jit(solution)/shard_map/all_gather | solution.py:86
  13.5 0.0 all-gather.2.cloned.1.call-update
  13.6 0.8 constant_dynamic-slice_fusion
  14.3 3.4 %all_gather.14 = bf16[224,128]{1,0:T(8,128)(2,1)S(1)} all-gather(bf16[112,128]{1,0:T(8,128)(2,1)S(1)} %constant_dynamic-slice_fusion), channel_id=1, replica_groups=mesh['yh'=2,'x'=4,'core'=2,'yl'=2,'z'=16] {'yl'}, dimensions={0}, use_global_device_ids=true | all-gather | bytes 86016 | tf_op jit(solution)/shard_map/all_gather | solution.py:90
  17.8 1.1 broadcast_in_dim.17
  18.8 16.4 %all-to-all-start = ((bf16[16,224,128]{2,1,0:T(8,128)(2,1)}), bf16[16,224,128]{2,1,0:T(8,128)(2,1)}, u32[]{:S(2)}, u32[]{:S(2)}) async-start(bf16[16,224,128]{2,1,0:T(8,128)(2,1)} %broadcast_in_dim.17), calls=%async_computation | async-start | bytes 1835008 | tf_op jit(solution)/shard_map/all_to_all | solution.py:30
  35.2 3.3 %reshape.135 = f32[192,2,16,112]{3,2,1,0:T(8,128)S(1)} reshape(bf16[3,64,3584]{2,1,0:T(8,128)(2,1)} %param.8) | data formatting | bytes 4128768 | tf_op jit(solution)/shard_map/convert_element_type | solution.py:19
  38.5 1.4 mul.58
  39.9 1.7 multiply_reduce_fusion
  41.6 0.1 rsqrt.20
  41.7 1.1 fusion.7
  42.9 0.0 copy-start.2
  42.9 1.6 copy.12
  44.5 3.2 %reshape.129 = bf16[192,3584]{1,0:T(8,128)(2,1)S(1)} reshape(bf16[192,16,2,112]{3,2,1,0:T(2,128)(2,1)S(1)} %copy.12) | data formatting | bytes 2752512 | tf_op jit(solution)/shard_map/reshape | solution.py:96
  47.7 0.1 iota_compare_fusion.2
  47.8 0.1 pad_maximum_fusion.1
  47.9 4.9 %collective-permute-start = (bf16[192,3712]{1,0:T(8,128)(2,1)S(1)}, bf16[192,3712]{1,0:T(8,128)(2,1)}, u32[]{:S(2)}, u32[]{:S(2)}) collective-permute-start(bf16[192,3712]{1,0:T(8,128)(2,1)S(1)} %pad_maximum_fusion.1), channel_id=1, source_target_pairs={{0,32},{32,0},{1,33},{33,1},{2,34},{34,2},{3,35},{35,3},{4,36},{36... | collective-permute-start | bytes 4276232 | tf_op jit(solution)/shard_map/ppermute | solution.py:119
  52.9 1.1 fusion.16
  54.0 1.8 fusion.18
  55.8 1.3 reshape.131
  57.1 0.9 copy.15
  58.0 1.3 reshape.132
  59.3 23.3 %all-to-all-done = bf16[16,224,128]{2,1,0:T(8,128)(2,1)} async-done(((bf16[16,224,128]{2,1,0:T(8,128)(2,1)}), bf16[16,224,128]{2,1,0:T(8,128)(2,1)}, u32[]{:S(2)}, u32[]{:S(2)}) %all-to-all-start) | async-done | bytes 917536 | tf_op jit(solution)/shard_map/all_to_all | solution.py:30
  82.7 1.4 convolution_convert_fusion
  84.1 3.6 %all_gather.15 = bf16[64,128]{1,0:T(8,128)(2,1)S(1)} all-gather(bf16[32,128]{1,0:T(8,128)(2,1)S(1)} %convolution_convert_fusion), channel_id=1, replica_groups=mesh['yh'=2,'x'=4,'core'=2,'yl'=2,'z'=16] {'yl'}, dimensions={0}, use_global_device_ids=true | all-gather | bytes 24576 | tf_op jit(solution)/shard_map/all_gather | solution.py:102
  87.7 0.8 broadcast_in_dim.18
  88.5 13.3 %all-to-all-start.1 = ((bf16[16,64,128]{2,1,0:T(8,128)(2,1)}), bf16[16,64,128]{2,1,0:T(8,128)(2,1)S(1)}, u32[]{:S(2)}, u32[]{:S(2)}) async-start(bf16[16,64,128]{2,1,0:T(8,128)(2,1)} %broadcast_in_dim.18), calls=%async_computation.1 | async-start | bytes 524288 | tf_op jit(solution)/shard_map/all_to_all | solution.py:30
  101.8 3.3 %collective-permute-start.1 = (bf16[3584,128]{1,0:T(8,128)(2,1)}, bf16[3584,128]{1,0:T(8,128)(2,1)}, u32[]{:S(2)}, u32[]{:S(2)}) collective-permute-start(bf16[3584,128]{1,0:T(8,128)(2,1)} %bitcast.3), channel_id=1, source_target_pairs={{0,64},{64,0},{128,192},{192,128},{1,65},{65,1},{129,193},{193,129... | collective-permute-start | bytes 2752520 | tf_op jit(solution)/shard_map/ppermute | solution.py:92
  105.1 0.8 pad_maximum_fusion.5.allowed
  105.9 3.2 %pad_maximum_fusion = bf16[384,3712]{1,0:T(8,128)(2,1)} fusion(bf16[192,3712]{1,0:T(8,128)(2,1)} %collective-permute-done, bf16[192,128]{1,0:T(8,128)(2,1)S(1)} %pad_convert_fusion, bf16[192,3584]{1,0:T(8,128)(2,1)S(1)} %reshape.129), kind=kLoop, calls=%fused_computation.1 | loop fusion | flops 8552448 | bytes 5701632 | tf_op jit(solution)/shard_map/concatenate | solution.py:119
  109.1 9.1 %all-to-all-done.1 = bf16[16,64,128]{2,1,0:T(8,128)(2,1)S(1)} async-done(((bf16[16,64,128]{2,1,0:T(8,128)(2,1)}), bf16[16,64,128]{2,1,0:T(8,128)(2,1)S(1)}, u32[]{:S(2)}, u32[]{:S(2)}) %all-to-all-start.1) | async-done | bytes 262176 | tf_op jit(solution)/shard_map/all_to_all | solution.py:30
  118.2 1.1 broadcast_in_dim.20
  119.3 4.2 %all-to-all-start.2 = ((bf16[4,1024,128]{2,1,0:T(8,128)(2,1)}), bf16[4,1024,128]{2,1,0:T(8,128)(2,1)S(1)}, u32[]{:S(2)}, u32[]{:S(2)}) async-start(bf16[4,1024,128]{2,1,0:T(8,128)(2,1)} %broadcast_in_dim.20), calls=%async_computation.2 | async-start | bytes 2097152 | tf_op jit(solution)/shard_map/all_to_all | solution.py:30
  123.5 1.8 broadcast_select_fusion.1
  125.3 0.6 copy-done.1
  125.9 0.9 fusion.11.step_keys.step_values
  126.8 7.3 %all-to-all-done.2 = bf16[4,1024,128]{2,1,0:T(8,128)(2,1)S(1)} async-done(((bf16[4,1024,128]{2,1,0:T(8,128)(2,1)}), bf16[4,1024,128]{2,1,0:T(8,128)(2,1)S(1)}, u32[]{:S(2)}, u32[]{:S(2)}) %all-to-all-start.2) | async-done | bytes 1048608 | tf_op jit(solution)/shard_map/all_to_all | solution.py:30
  134.0 0.1 slice_bitcast_fusion.1
  134.1 0.1 pad_maximum_fusion.3
  134.2 19.8 %all-gather.2.cloned.1.call-done = bf16[3584,896]{1,0:T(8,128)(2,1)} async-done(((bf16[224,896]{1,0:T(8,128)(2,1)}), bf16[3584,896]{1,0:T(8,128)(2,1)}) %all-gather.2.cloned.1.call-update) | async-done | bytes 6422544 | tf_op jit(solution)/shard_map/all_gather | solution.py:87
  154.0 6.7 %fusion.8.query = bf16[384,896]{1,0:T(8,128)(2,1)S(1)} fusion(bf16[3584,896]{1,0:T(8,128)(2,1)} %all-gather.2.cloned.1.call-done, bf16[384,3712]{1,0:T(8,128)(2,1)} %pad_maximum_fusion), kind=kOutput, calls=%fused_computation.12 | convolution fusion | flops 2466594816 | bytes 9863168 | tf_op jit(solution)/shard_map/dot_general | solution.py:25
  160.7 15.1 %shard_map.73 = bf16[384,896]{1,0:T(8,128)(2,1)S(1)} custom-call(bf16[384,896]{1,0:T(8,128)(2,1)S(1)} %fusion.8.query, bf16[2048,128]{1,0:T(8,128)(2,1)S(1)} %get-tuple-element.15.keys, bf16[2048,128]{1,0:T(8,128)(2,1)S(1)} %get-tuple-element.16.values, bf16[384,256]{1,0:T(8,128)(2,1)S(1)} %fusion.11.step_keys.step_values, ...), custom_call_target="tpu_custom_call" | custom-call | flops 2818572288 | bytes 1376256 | tf_op jit(solution)/shard_map/pallas_call | solution.py:57
  175.8 4.6 %collective-permute-start.2 = (bf16[192,896]{1,0:T(8,128)(2,1)S(1)}, bf16[192,896]{1,0:T(8,128)(2,1)S(1)}, u32[]{:S(2)}, u32[]{:S(2)}) collective-permute-start(bf16[192,896]{1,0:T(8,128)(2,1)S(1)} %slice.38), channel_id=1, source_target_pairs={{0,32},{32,0},{1,33},{33,1},{2,34},{34,2},{3,35},{35,3},{4,36},{36... | collective-permute-start | bytes 1032200 | tf_op jit(solution)/shard_map/ppermute | solution.py:130
  180.5 1.3 collective-permute-done.2
  181.7 0.1 broadcast_select_fusion.4
  181.8 0.1 pad_maximum_fusion.2
  181.8 1.0 broadcast_select_fusion.2
  (17 shorter events, 0.2 us)
Async XLA Ops:
  6.5 1.0 copy-start
  6.5 147.5 %all-gather.2.cloned.1.call-start = ((), (), s32[]{:S(2)}) async-start(), calls=%async_computation.3 | async-start | bytes 6823936 | tf_op jit(solution)/shard_map/all_gather | solution.py:87
  18.8 63.8 %all-to-all-start = ((bf16[16,224,128]{2,1,0:T(8,128)(2,1)}), bf16[16,224,128]{2,1,0:T(8,128)(2,1)}, u32[]{:S(2)}, u32[]{:S(2)}) async-start(bf16[16,224,128]{2,1,0:T(8,128)(2,1)} %broadcast_in_dim.17), calls=%async_computation | async-start | bytes 1835008 | tf_op jit(solution)/shard_map/all_to_all | solution.py:30
  42.8 4.8 %copy-start.4 = (s32[3]{0:T(128)S(1)}, s32[3]{0:T(128)}, u32[]{:S(2)}) copy-start(s32[3]{0:T(128)} %param.12) | copy-start | bytes 40
  42.9 4.9 %copy-start.2 = (s32[3,64,64]{2,1,0:T(8,128)S(1)}, s32[3,64,64]{2,1,0:T(8,128)}, u32[]{:S(2)}) copy-start(s32[3,64,64]{2,1,0:T(8,128)} %param.13) | copy-start | bytes 147460
  44.5 9.5 %copy-start.3 = (f32[3584]{0:T(1024)S(1)}, f32[3584]{0:T(1024)}, u32[]{:S(2)}) copy-start(f32[3584]{0:T(1024)} %param.9) | copy-start | bytes 43012
  47.9 57.1 %collective-permute-start = (bf16[192,3712]{1,0:T(8,128)(2,1)S(1)}, bf16[192,3712]{1,0:T(8,128)(2,1)}, u32[]{:S(2)}, u32[]{:S(2)}) collective-permute-start(bf16[192,3712]{1,0:T(8,128)(2,1)S(1)} %pad_maximum_fusion.1), channel_id=1, source_target_pairs={{0,32},{32,0},{1,33},{33,1},{2,34},{34,2},{3,35},{35,3},{4,36},{36... | collective-permute-start | bytes 4276232 | tf_op jit(solution)/shard_map/ppermute | solution.py:119
  88.5 29.7 %all-to-all-start.1 = ((bf16[16,64,128]{2,1,0:T(8,128)(2,1)}), bf16[16,64,128]{2,1,0:T(8,128)(2,1)S(1)}, u32[]{:S(2)}, u32[]{:S(2)}) async-start(bf16[16,64,128]{2,1,0:T(8,128)(2,1)} %broadcast_in_dim.18), calls=%async_computation.1 | async-start | bytes 524288 | tf_op jit(solution)/shard_map/all_to_all | solution.py:30
  101.8 21.7 %collective-permute-start.1 = (bf16[3584,128]{1,0:T(8,128)(2,1)}, bf16[3584,128]{1,0:T(8,128)(2,1)}, u32[]{:S(2)}, u32[]{:S(2)}) collective-permute-start(bf16[3584,128]{1,0:T(8,128)(2,1)} %bitcast.3), channel_id=1, source_target_pairs={{0,64},{64,0},{128,192},{192,128},{1,65},{65,1},{129,193},{193,129... | collective-permute-start | bytes 2752520 | tf_op jit(solution)/shard_map/ppermute | solution.py:92
  119.3 14.8 %all-to-all-start.2 = ((bf16[4,1024,128]{2,1,0:T(8,128)(2,1)}), bf16[4,1024,128]{2,1,0:T(8,128)(2,1)S(1)}, u32[]{:S(2)}, u32[]{:S(2)}) async-start(bf16[4,1024,128]{2,1,0:T(8,128)(2,1)} %broadcast_in_dim.20), calls=%async_computation.2 | async-start | bytes 2097152 | tf_op jit(solution)/shard_map/all_to_all | solution.py:30
  123.5 2.4 %copy-start.1 = (bf16[384,3712]{1,0:T(8,128)(2,1)S(1)}, bf16[384,3712]{1,0:T(8,128)(2,1)}, u32[]{:S(2)}) copy-start(bf16[384,3712]{1,0:T(8,128)(2,1)} %pad_maximum_fusion) | copy-start | bytes 8552452
  175.8 5.9 %collective-permute-start.2 = (bf16[192,896]{1,0:T(8,128)(2,1)S(1)}, bf16[192,896]{1,0:T(8,128)(2,1)S(1)}, u32[]{:S(2)}, u32[]{:S(2)}) collective-permute-start(bf16[192,896]{1,0:T(8,128)(2,1)S(1)} %slice.38), channel_id=1, source_target_pairs={{0,32},{32,0},{1,33},{33,1},{2,34},{34,2},{3,35},{35,3},{4,36},{36... | collective-permute-start | bytes 1032200 | tf_op jit(solution)/shard_map/ppermute | solution.py:130
Sparse Core Ops, SparseCore 0:
  13.7 140.2 all-gather.1

commit v2 on v1

v2 whole, which is shorter than its diff:
```python
import functools
import math

import jax
import jax.numpy as jnp
from jax import lax
from jax.experimental import pallas as pl
from jax.experimental.pallas import tpu as pltpu
from jax.sharding import Mesh
from jax.sharding import PartitionSpec as P

HEAD_SIZE = 128
NEG_FILL = -1e30
AXES = ("yh", "x", "core", "yl", "z")
SWAP = [(0, 1), (1, 0)]
CHUNK = 1024
DEPTH = 256


def rms_norm(hidden_rows, norm_gain):
    widened = hidden_rows.astype(jnp.float32)
    inverse = lax.rsqrt(jnp.mean(widened * widened, axis=-1, keepdims=True) + 1e-06)
    return (widened * inverse * norm_gain).astype(jnp.bfloat16)


def dot(a, b):
    return jnp.dot(a, b, preferred_element_type=jnp.float32)


def spread(block, axis):
    size = math.prod(lax.axis_size(one) for one in (axis if isinstance(axis, tuple) else (axis,)))
    return lax.all_to_all(jnp.broadcast_to(block[None], (size,) + block.shape), axis, 0, 0, tiled=True)


def attend_sample(query, keys, values, step_keys, step_values, seen, chunk):
    scale = math.log2(math.e) / math.sqrt(HEAD_SIZE)
    contract = (((1,), (1,)), ((), ()))
    near = lax.dot_general(query, step_keys, contract, preferred_element_type=jnp.float32)
    near = jnp.where(seen, near, NEG_FILL)
    starts = range(0, keys.shape[0], chunk)
    far = [
        lax.dot_general(query, keys[at : at + chunk], contract, preferred_element_type=jnp.float32) for at in starts
    ]
    top = near.max(-1, keepdims=True)
    for scores in far:
        top = jnp.maximum(top, scores.max(-1, keepdims=True))
    top = top * scale
    weights = jnp.exp2(near * scale - top)
    total = weights.sum(-1, keepdims=True)
    attended = dot(weights.astype(jnp.bfloat16), step_values)
    for at, scores in zip(starts, far):
        weights = jnp.exp2(scores * scale - top)
        total = total + weights.sum(-1, keepdims=True)
        attended = attended + dot(weights.astype(jnp.bfloat16), values[at : at + chunk])
    return (attended / total).astype(jnp.bfloat16)


def attend_kernel(
    chunks, slots, low, high, low_weights, high_weights, context, step_keys, step_values, allowed, out, *scratch
):
    total, query, keys, values = scratch
    step = pl.program_id(0)
    heads = query.shape[1] // HEAD_SIZE

    @pl.when(step == 0)
    def _():
        total[...] = jnp.zeros_like(total)
        count, quarter = context.shape[1], HEAD_SIZE // 2
        for hi in range(context.shape[0] // 4):
            for x in range(4):
                to, lane = (keys, values)[x // 2], x % 2 * quarter
                for side in range(2):
                    at = (hi * 2 + side) * count
                    to[at : at + count, lane : lane + quarter] = context[
                        hi * 4 + x, :, side * quarter : (side + 1) * quarter
                    ]

    @pl.when(step < chunks)
    def _():
        total[...] += dot(low[...], low_weights[...]) + dot(high[...], high_weights[...])

    @pl.when(step == chunks - 1)
    def _():
        query[...] = total[...].astype(jnp.bfloat16)

    @pl.when(step >= chunks)
    def _():
        rows = out.shape[0]
        first = (step - chunks) * rows
        for at in range(0, rows, slots):
            here = slice(at, at + slots)
            own = query[pl.ds(pl.multiple_of(first + at, slots), slots), :]
            own = jnp.concatenate([own[:, h * HEAD_SIZE : (h + 1) * HEAD_SIZE] for h in range(heads)], 0)
            seen = jnp.concatenate([allowed[here, :slots].astype(jnp.float32)] * heads, 0) > 0.5
            result = attend_sample(own, keys, values, step_keys[here], step_values[here], seen, CHUNK)
            out[here, :] = jnp.concatenate([result[h * slots : (h + 1) * slots] for h in range(heads)], 1)


def attend(normed, query_weights, context, step_keyval, allowed, slots):
    rows, features = normed.shape
    half, cols = query_weights.shape[0], query_weights.shape[1] // 2
    tokens = context.shape[0] * context.shape[1] // 2
    chunks = half // DEPTH
    at_once = 2 * slots
    project_at = lambda i: jnp.minimum(i, chunks - 1)
    attend_at = lambda i: jnp.maximum(i - chunks, 0)
    return pl.pallas_call(
        functools.partial(attend_kernel, chunks, slots),
        grid=(chunks + rows // at_once,),
        in_specs=[
            pl.BlockSpec((rows, DEPTH), lambda i: (0, project_at(i))),
            pl.BlockSpec((rows, DEPTH), lambda i: (0, chunks + project_at(i))),
            pl.BlockSpec((DEPTH, cols), lambda i: (project_at(i), 0)),
            pl.BlockSpec((DEPTH, cols), lambda i: (project_at(i), 1)),
            pl.BlockSpec(context.shape, lambda i: (0, 0, 0)),
            pl.BlockSpec((at_once, HEAD_SIZE), lambda i: (attend_at(i), 0)),
            pl.BlockSpec((at_once, HEAD_SIZE), lambda i: (attend_at(i), 1)),
            pl.BlockSpec((at_once, allowed.shape[1]), lambda i: (attend_at(i), 0)),
        ],
        out_specs=pl.BlockSpec((at_once, cols), lambda i: (attend_at(i), 0)),
        out_shape=jax.ShapeDtypeStruct((rows, cols), jnp.bfloat16),
        scratch_shapes=[pltpu.VMEM((rows, cols), jnp.float32), pltpu.VMEM((rows, cols), jnp.bfloat16)]
        + [pltpu.VMEM((tokens, HEAD_SIZE), jnp.bfloat16)] * 2,
        compiler_params=pltpu.CompilerParams(vmem_limit_bytes=44 * 2**20),
        cost_estimate=pl.CostEstimate(
            flops=4 * rows * cols * tokens + 2 * rows * cols * features,
            bytes_accessed=2 * features * cols,
            transcendentals=rows * tokens * cols // HEAD_SIZE,
        ),
    )(normed, normed, query_weights, query_weights, context, step_keyval, step_keyval, allowed)


def project(rows, packed):
    features, width = rows.shape[1] // 2, packed.shape[1] // 2
    return dot(rows[:, :features], packed[:, :width]) + dot(rows[:, features:], packed[:, width:])


def pack(block):
    half = block.shape[-2] // 2
    return jnp.concatenate([block[..., :half, :], block[..., half:, :]], -1)


def local(ctx_hidden, step_hidden, norm_gain, w_query, w_keyval, step_lengths, step_mask):
    samples, slots, features = step_hidden.shape
    rows = samples * slots
    kv_heads = w_keyval.shape[1] // (2 * HEAD_SIZE)
    cols = w_query.shape[1] // kv_heads
    chips = lax.axis_size("x")
    quarter = 2 * HEAD_SIZE // chips
    core, x = lax.axis_index("core"), lax.axis_index("x")

    own_query = lax.dynamic_slice_in_dim(w_query, core * cols, cols, 1)
    start = (x // 2) * kv_heads * HEAD_SIZE + core * HEAD_SIZE + (x % 2) * quarter
    own_kv = lax.dynamic_slice_in_dim(w_keyval, start, quarter, 1)
    pair = lax.all_gather(jnp.concatenate([own_query, own_kv], 1), "yl", axis=0)
    pair_query = jnp.concatenate([pair[0, :, :cols], pair[1, :, :cols]], 1)
    pair_kv = jnp.concatenate([pair[0, :, cols:], pair[1, :, cols:]], 1)
    pair_query, pair_kv, step_hidden, ctx_hidden = lax.optimization_barrier(
        (pair_query, pair_kv, step_hidden, ctx_hidden)
    )
    query_weights = lax.all_gather(pair_query, "z", axis=0, tiled=True)
    yh = lax.axis_index("yh")
    rows_half = pair_kv.shape[0] // 2
    half_kv = spread(lax.dynamic_slice_in_dim(pair_kv, yh * rows_half, rows_half, 0), "z")
    rest_kv = lax.ppermute(half_kv, "yh", SWAP)
    low_first = yh == 0
    part_kv = jnp.concatenate([jnp.where(low_first, half_kv, rest_kv), jnp.where(low_first, rest_kv, half_kv)], 1)
    part_kv = part_kv.reshape(-1, 2 * quarter)

    own_tokens = ctx_hidden.shape[0] // 2
    own_context = lax.dynamic_slice_in_dim(ctx_hidden, yh * own_tokens, own_tokens, 0)
    context = project(rms_norm(own_context, norm_gain), part_kv).astype(jnp.bfloat16)
    context = lax.all_gather(pack(context), "yl", axis=0, tiled=True)
    context = spread(spread(context, "z").reshape(-1, 2 * quarter), ("yh", "x"))

    positions = lax.iota(jnp.int32, slots)
    causal = positions[None, :] <= positions[:, None]
    diagonal = positions[None, :] == positions[:, None]
    allowed = (
        causal[None]
        & (diagonal[None] | (step_mask == 1))
        & (positions[None, None, :] < step_lengths[:, None, None])
    )
    allowed = jnp.pad(allowed.astype(jnp.bfloat16).reshape(rows, slots), ((0, 0), (0, HEAD_SIZE - slots)))
    allowed = jnp.concatenate([allowed, lax.ppermute(allowed, "core", SWAP)], 0)
    normed_step = rms_norm(step_hidden.reshape(rows, features), norm_gain)
    both_rows = jnp.concatenate([normed_step, lax.ppermute(normed_step, "core", SWAP)], 0)

    turns = [part_kv] + [
        lax.ppermute(part_kv, "x", [(i, (i - turn) % chips) for i in range(chips)]) for turn in range(1, chips)
    ]
    kv_weights = jnp.concatenate(
        [
            jnp.concatenate([one[:, :quarter] for one in turns], 1),
            jnp.concatenate([one[:, quarter:] for one in turns], 1),
        ],
        0,
    )
    step_keyval = dot(both_rows, kv_weights).astype(jnp.bfloat16)
    step_keyval = jnp.concatenate([step_keyval, step_keyval], 1)
    step_keyval = lax.dynamic_slice_in_dim(step_keyval, (chips - x) % chips * quarter, chips * quarter, 1)
    attended = attend(both_rows, query_weights, context, step_keyval, allowed, slots)

    mine, theirs = attended[:rows], lax.ppermute(attended[rows:], "core", SWAP)
    first = core == 0
    result = jnp.concatenate([jnp.where(first, mine, theirs), jnp.where(first, theirs, mine)], 1)
    result = result.reshape(samples, slots, kv_heads * cols)
    live_rows = positions[None, :] < step_lengths[:, None]
    return jnp.where(live_rows[:, :, None], result, jnp.bfloat16(0.0))


def solution(mesh):
    five = Mesh(mesh.devices.reshape(2, 4, 2, 2, 16), AXES)
    dev, everywhere = ("yl", "z"), AXES
    placed = (
        P(dev, None),
        P(everywhere, None, None),
        P(),
        P(dev, None),
        P(dev, None),
        P(everywhere),
        P(everywhere, None, None),
    )
    return jax.shard_map(
        local, mesh=five, in_specs=placed, out_specs=P(everywhere, None, None), check_vma=False
    )
```

time: 191 us -> 152 us (0.80)
  waiting for transfers between devices: 60.8 us -> 22.6 us
  starting transfers between devices: 46.8 us -> 58.7 us
  local copies, waits for them, and re-layouts: 18.5 us -> 12.8 us
  other arithmetic: 12.8 us -> 9.13 us
  blocking collectives: 13 us -> 9.86 us
  Pallas kernels: 15.1 us -> 17.8 us
  matrix products: 8.96 us -> 6.65 us
    all_to_all x3, waiting for transfers between devices: 39.7 us -> 15.3 us  [spread(): lax.all_to_all(jnp.broadcast_to(block[None], (size,) + block.shape), axis...]
    all_gather x1, waiting for transfers between devices: 19.8 us -> 3.66 us  [local(): query_weights = lax.all_gather(pair_query, 'z', axis=0, tiled=True)]
    ppermute x2 -> x6, starting transfers between devices: 8.22 us -> 19.8 us  [the longest x3 9.32 us: local(): lax.ppermute(part_kv, 'x', [(i, (i - turn) % chips) for i in range(chips)])]
    slice x0 -> x5, local copies, waits for them, and re-layouts: none -> 8.24 us  [the longest x3 5.85 us: local(): one[:, :quarter]]
    reshape x4 -> x0, local copies, waits for them, and re-layouts: 6.67 us -> none  [reorder(): normed.reshape(count, 2, features // share // 2, share).swapaxes(1, 2)]
    convert_element_type x1 -> x0, local copies, waits for them, and re-layouts: 3.26 us -> none  [rms_norm(): widened = hidden_rows.astype(jnp.float32)]
    all_gather x3 -> x2, blocking collectives: 13 us -> 9.86 us  [the longest x1 6.2 us: local(): pair = lax.all_gather(jnp.concatenate([own_query, own_kv], 1), 'yl', axis=0)]
    pallas_call x1, Pallas kernels: 15.1 us -> 17.8 us  [attend(): pl.pallas_call(functools.partial(attend_kernel, chunks, slots), grid=(chu...]
  transfers between devices with their start and end apart: 7 -> 11, of which waited for: 5 -> 6; matrix products, arithmetic and copies ran while one was open for 16% -> 16% of each run, Pallas kernels for 0% -> 0%
where the time goes in v2:
time: 152 us; the launch traced here: 151 us
  starting transfers between devices  58.7 us (39%)
  waiting for transfers between devices  22.6 us (15%)
  Pallas kernels  17.8 us (12%)
  between operations  13.7 us (9%)
  local copies, waits for them, and re-layouts  12.8 us (8%)
  blocking collectives  9.86 us (6%)
  other arithmetic  9.13 us (6%)
  matrix products  6.65 us (4%)
    all_to_all x3, starting transfers between devices, spread(): lax.all_to_all(jnp.broadcast_to(block[None], (size,) + block.shape), axis...  32.6 us
    pallas_call x1, Pallas kernels, attend(): pl.pallas_call(functools.partial(attend_kernel, chunks, slots), grid=(chu...  17.8 us
    all_to_all x3, waiting for transfers between devices, spread(): lax.all_to_all(jnp.broadcast_to(block[None], (size,) + block.shape), axis...  15.3 us
    ppermute x3, starting transfers between devices, local(): lax.ppermute(part_kv, 'x', [(i, (i - turn) % chips) for i in range(chips)])  9.32 us
    dot_general x3, matrix products, dot(): return jnp.dot(a, b, preferred_element_type=jnp.float32)  6.65 us
    ppermute x1, starting transfers between devices, local(): lax.ppermute(attended[rows:], 'core', SWAP)  6.24 us
    all_gather x1, blocking collectives, local(): pair = lax.all_gather(jnp.concatenate([own_query, own_kv], 1), 'yl', axis=0)  6.2 us
    slice x3, local copies, waits for them, and re-layouts, local(): one[:, :quarter]  5.85 us
  transfers between devices with their start and end apart: 11, of which 6 were waited for; matrix products, arithmetic and copies ran while one was open for 16% of the time, Pallas kernels for 0%

profile of v2, /device:TPU:1, one launch (start us, length us, event | category | flops | bytes accessed | tf_op | source)
XLA Modules:
  0.0 151.2 jit_solution(13847481305170273928)
XLA Ops:
  6.5 1.0 constant_dynamic-slice_fusion.1
  7.5 0.0 copy-done
  7.6 6.2 %all-gather = bf16[224,960]{1,0:T(8,128)(2,1)S(1)} all-gather(bf16[112,960]{1,0:T(8,128)(2,1)S(1)} %pad_maximum_fusion.4), channel_id=2, replica_groups=mesh['yh'=2,'x'=4,'core'=2,'yl'=2,'z'=16] {'yl'}, dimensions={0}, use_global_device_ids=true | all-gather | bytes 645120 | tf_op jit(solution)/shard_map/all_gather | solution.py:155
  13.9 0.1 pad_maximum_fusion.6
  13.9 0.8 pad_maximum_fusion.3
  14.7 0.0 all-gather.3.cloned.1.call-update
  14.8 0.7 broadcast_in_dim.17
  15.5 16.7 %all-to-all-start = ((bf16[16,56,128]{2,1,0:T(8,128)(2,1)}), bf16[16,56,128]{2,1,0:T(8,128)(2,1)S(1)}, u32[]{:S(2)}, u32[]{:S(2)}) async-start(bf16[16,56,128]{2,1,0:T(8,128)(2,1)} %broadcast_in_dim.17), calls=%async_computation | async-start | bytes 458752 | tf_op jit(solution)/shard_map/all_to_all | solution.py:32
  32.2 0.4 multiply_reduce_fusion
  32.6 0.1 rsqrt.20
  32.7 0.4 fusion.1
  33.1 3.7 %collective-permute-start = (bf16[192,3584]{1,0:T(8,128)(2,1)S(1)}, bf16[192,3584]{1,0:T(8,128)(2,1)}, u32[]{:S(2)}, u32[]{:S(2)}) collective-permute-start(bf16[192,3584]{1,0:T(8,128)(2,1)S(1)} %fusion.1), channel_id=1, source_target_pairs={{0,32},{32,0},{1,33},{33,1},{2,34},{34,2},{3,35},{35,3},{4,36},{36... | collective-permute-start | bytes 4128776 | tf_op jit(solution)/shard_map/ppermute | solution.py:187
  36.9 0.1 iota_compare_fusion.2
  37.0 1.9 %collective-permute-start.5 = (bf16[192,128]{1,0:T(8,128)(2,1)S(1)}, bf16[192,128]{1,0:T(8,128)(2,1)S(1)}, u32[]{:S(2)}, u32[]{:S(2)}) collective-permute-start(bf16[192,128]{1,0:T(8,128)(2,1)S(1)} %pad_convert_fusion), channel_id=1, source_target_pairs={{0,32},{32,0},{1,33},{33,1},{2,34},{34,2},{3,35},{35,3},{4,36},{36... | collective-permute-start | bytes 147464 | tf_op jit(solution)/shard_map/ppermute | solution.py:185
  38.9 1.1 fusion.22
  40.0 4.8 %all-to-all-done = bf16[16,56,128]{2,1,0:T(8,128)(2,1)S(1)} async-done(((bf16[16,56,128]{2,1,0:T(8,128)(2,1)}), bf16[16,56,128]{2,1,0:T(8,128)(2,1)S(1)}, u32[]{:S(2)}, u32[]{:S(2)}) %all-to-all-start) | async-done | bytes 229408 | tf_op jit(solution)/shard_map/all_to_all | solution.py:32
  44.8 4.8 %collective-permute-start.1 = (bf16[16,56,128]{2,1,0:T(8,128)(2,1)S(1)}, bf16[16,56,128]{2,1,0:T(8,128)(2,1)S(1)}, u32[]{:S(2)}, u32[]{:S(2)}) collective-permute-start(bf16[16,56,128]{2,1,0:T(8,128)(2,1)S(1)} %all-to-all-done), channel_id=1, source_target_pairs={{0,256},{256,0},{1,257},{257,1},{2,258},{258,2},{3,259},{259,3},{4... | collective-permute-start | bytes 688136 | tf_op jit(solution)/shard_map/ppermute | solution.py:165
  49.7 1.1 fusion.24
  50.8 2.4 %collective-permute-done.1 = bf16[16,56,128]{2,1,0:T(8,128)(2,1)S(1)} collective-permute-done((bf16[16,56,128]{2,1,0:T(8,128)(2,1)S(1)}, bf16[16,56,128]{2,1,0:T(8,128)(2,1)S(1)}, u32[]{:S(2)}, u32[]{:S(2)}) %collective-permute-start.1) | collective-permute-done | bytes 229408 | tf_op jit(solution)/shard_map/ppermute | solution.py:165
  53.2 0.8 pad_maximum_fusion.2
  54.0 4.4 %collective-permute-start.2 = (bf16[1792,128]{1,0:T(8,128)(2,1)}, bf16[1792,128]{1,0:T(8,128)(2,1)}, u32[]{:S(2)}, u32[]{:S(2)}) collective-permute-start(bf16[1792,128]{1,0:T(8,128)(2,1)} %bitcast.6), channel_id=1, source_target_pairs={{0,192},{64,0},{128,64},{192,128},{1,193},{65,1},{129,65},{193,129... | collective-permute-start | bytes 1376264 | tf_op jit(solution)/shard_map/ppermute | solution.py:190
  58.4 2.4 %collective-permute-start.3 = (bf16[1792,128]{1,0:T(8,128)(2,1)}, bf16[1792,128]{1,0:T(8,128)(2,1)}, u32[]{:S(2)}, u32[]{:S(2)}) collective-permute-start(bf16[1792,128]{1,0:T(8,128)(2,1)} %bitcast.6), channel_id=1, source_target_pairs={{0,128},{64,192},{128,0},{192,64},{1,129},{65,193},{129,1},{193,65... | collective-permute-start | bytes 1376264 | tf_op jit(solution)/shard_map/ppermute | solution.py:190
  60.8 2.5 %collective-permute-start.4 = (bf16[1792,128]{1,0:T(8,128)(2,1)}, bf16[1792,128]{1,0:T(8,128)(2,1)}, u32[]{:S(2)}, u32[]{:S(2)}) collective-permute-start(bf16[1792,128]{1,0:T(8,128)(2,1)} %bitcast.6), channel_id=1, source_target_pairs={{0,64},{64,128},{128,192},{192,0},{1,65},{65,129},{129,193},{193,1... | collective-permute-start | bytes 1376264 | tf_op jit(solution)/shard_map/ppermute | solution.py:190
  63.3 1.2 fusion.27
  64.6 1.4 fusion.21
  65.9 0.1 pad_maximum_fusion.7
  66.0 3.7 %all_gather.15 = bf16[32,128]{1,0:T(8,128)(2,1)S(1)} all-gather(bf16[16,128]{1,0:T(8,128)(2,1)S(1)} %pad_maximum_fusion.7), channel_id=1, replica_groups=mesh['yh'=2,'x'=4,'core'=2,'yl'=2,'z'=16] {'yl'}, dimensions={0}, use_global_device_ids=true | all-gather | bytes 12288 | tf_op jit(solution)/shard_map/all_gather | solution.py:173
  69.7 0.7 broadcast_in_dim.18
  70.3 9.7 %all-to-all-start.1 = ((bf16[16,32,128]{2,1,0:T(8,128)(2,1)}), bf16[16,32,128]{2,1,0:T(8,128)(2,1)S(1)}, u32[]{:S(2)}, u32[]{:S(2)}) async-start(bf16[16,32,128]{2,1,0:T(8,128)(2,1)} %broadcast_in_dim.18), calls=%async_computation.1 | async-start | bytes 262144 | tf_op jit(solution)/shard_map/all_to_all | solution.py:32
  80.1 2.4 %fusion.32 = (bf16[1792,64]{1,0:T(8,128)(2,1)}, bf16[1792,64]{1,0:T(8,128)(2,1)}) fusion(bf16[1792,128]{1,0:T(8,128)(2,1)} %bitcast.6), kind=kLoop, calls=%fused_computation.64 | loop fusion | bytes 917504 | tf_op jit(solution)/shard_map/slice | solution.py:135
  82.5 1.9 %pad_maximum_fusion.low.high = bf16[384,3584]{1,0:T(8,128)(2,1)S(1)} fusion(bf16[192,3584]{1,0:T(8,128)(2,1)} %collective-permute-done, bf16[192,3584]{1,0:T(8,128)(2,1)} %copy-done.3), kind=kLoop, calls=%fused_computation | loop fusion | flops 5505024 | bytes 5505024 | tf_op jit(solution)/shard_map/concatenate | solution.py:187
  84.4 2.3 %fusion.33 = (bf16[1792,64]{1,0:T(8,128)(2,1)}, bf16[1792,64]{1,0:T(8,128)(2,1)}) fusion(bf16[1792,128]{1,0:T(8,128)(2,1)} %collective-permute-done.2), kind=kLoop, calls=%fused_computation.65 | loop fusion | bytes 917504 | tf_op jit(solution)/shard_map/slice | solution.py:194
  86.7 2.2 %fusion.34 = (bf16[1792,64]{1,0:T(8,128)(2,1)}, bf16[1792,64]{1,0:T(8,128)(2,1)}) fusion(bf16[1792,128]{1,0:T(8,128)(2,1)} %collective-permute-done.3), kind=kLoop, calls=%fused_computation.66 | loop fusion | bytes 917504 | tf_op jit(solution)/shard_map/slice | solution.py:194
  88.9 4.2 %all-to-all-done.1 = bf16[16,32,128]{2,1,0:T(8,128)(2,1)S(1)} async-done(((bf16[16,32,128]{2,1,0:T(8,128)(2,1)}), bf16[16,32,128]{2,1,0:T(8,128)(2,1)S(1)}, u32[]{:S(2)}, u32[]{:S(2)}) %all-to-all-start.1) | async-done | bytes 131104 | tf_op jit(solution)/shard_map/all_to_all | solution.py:32
  93.1 1.1 broadcast_in_dim.20
  94.2 6.2 %all-to-all-start.2 = ((bf16[8,512,128]{2,1,0:T(8,128)(2,1)}), bf16[8,512,128]{2,1,0:T(8,128)(2,1)}, u32[]{:S(2)}, u32[]{:S(2)}) async-start(bf16[8,512,128]{2,1,0:T(8,128)(2,1)} %broadcast_in_dim.20), calls=%async_computation.2 | async-start | bytes 2097152 | tf_op jit(solution)/shard_map/all_to_all | solution.py:32
  100.4 1.4 fusion.35
  101.8 4.1 %fusion.18 = bf16[384,256]{1,0:T(8,128)(2,1)S(1)} fusion(bf16[1792,64]{1,0:T(8,128)(2,1)S(1)} %get-tuple-element.22, bf16[1792,64]{1,0:T(8,128)(2,1)} %get-tuple-element.20, bf16[1792,64]{1,0:T(8,128)(2,1)} %get-tuple-element.18, bf16[1792,64]{1,0:T(8,128)(2,1)} %get-tuple-element.16, bf16[1792,64]{1,0:T(8,128)(2,1)S(1)} %get-tuple-element.21, ...), kind=kOutput, calls=%fused_computation.21 | convolution fusion | flops 724926464 | bytes 4784128 | tf_op jit(solution)/shard_map/dot_general | solution.py:27
  105.9 0.2 fusion.25.step_keys.step_values
  106.1 6.3 %all-to-all-done.2.context = bf16[8,512,128]{2,1,0:T(8,128)(2,1)} async-done(((bf16[8,512,128]{2,1,0:T(8,128)(2,1)}), bf16[8,512,128]{2,1,0:T(8,128)(2,1)}, u32[]{:S(2)}, u32[]{:S(2)}) %all-to-all-start.2) | async-done | bytes 1048608 | tf_op jit(solution)/shard_map/all_to_all | solution.py:32
  112.4 3.7 %all-gather.3.cloned.1.call-done.low_weights.high_weights = bf16[1792,1792]{1,0:T(8,128)(2,1)} async-done(((bf16[112,1792]{1,0:T(8,128)(2,1)}), bf16[1792,1792]{1,0:T(8,128)(2,1)}) %all-gather.3.cloned.1.call-update) | async-done | bytes 6422544 | tf_op jit(solution)/shard_map/all_gather | solution.py:161
  116.1 17.8 %shard_map.73 = bf16[384,896]{1,0:T(8,128)(2,1)S(1)} custom-call(bf16[384,3584]{1,0:T(8,128)(2,1)S(1)} %pad_maximum_fusion.low.high, bf16[384,3584]{1,0:T(8,128)(2,1)S(1)} %pad_maximum_fusion.low.high, bf16[1792,1792]{1,0:T(8,128)(2,1)} %all-gather.3.cloned.1.call-done.low_weights.high_weights, ...), custom_call_target="tpu_custom_call" | custom-call | flops 5284823040 | bytes 6422528 | tf_op jit(solution)/shard_map/pallas_call | solution.py:107
  133.9 0.8 copy-done.1
  134.7 6.2 %collective-permute-start.6 = (bf16[192,896]{1,0:T(8,128)(2,1)S(1)}, bf16[192,896]{1,0:T(8,128)(2,1)S(1)}, u32[]{:S(2)}, u32[]{:S(2)}) collective-permute-start(bf16[192,896]{1,0:T(8,128)(2,1)S(1)} %slice.91), channel_id=1, source_target_pairs={{0,32},{32,0},{1,33},{33,1},{2,34},{34,2},{3,35},{35,3},{4,36},{36... | collective-permute-start | bytes 1032200 | tf_op jit(solution)/shard_map/ppermute | solution.py:204
  141.0 1.3 collective-permute-done.6
  142.2 1.1 broadcast_select_fusion.2
  143.3 0.1 pad_maximum_fusion.1
  143.3 1.0 broadcast_select_fusion
  (32 shorter events, 0.3 us)
Async XLA Ops:
  6.5 1.0 copy-start
  6.5 25.7 %copy-start.2 = (bf16[3,64,3584]{2,1,0:T(8,128)(2,1)S(1)}, bf16[3,64,3584]{2,1,0:T(8,128)(2,1)}, u32[]{:S(2)}) copy-start(bf16[3,64,3584]{2,1,0:T(8,128)(2,1)} %param.8) | copy-start | bytes 4128772
  6.5 109.5 %all-gather.3.cloned.1.call-start = ((), (), s32[]{:S(2)}) async-start(), calls=%async_computation.3 | async-start | bytes 6823936 | tf_op jit(solution)/shard_map/all_gather | solution.py:161
  7.6 25.1 %copy-start.5 = (f32[3584]{0:T(1024)S(1)}, f32[3584]{0:T(1024)}, u32[]{:S(2)}) copy-start(f32[3584]{0:T(1024)} %param.9) | copy-start | bytes 43012
  14.7 22.1 %copy-start.6 = (s32[3]{0:T(128)S(1)}, s32[3]{0:T(128)}, u32[]{:S(2)}) copy-start(s32[3]{0:T(128)} %param.12) | copy-start | bytes 40
  14.7 22.2 %copy-start.4 = (s32[3,64,64]{2,1,0:T(8,128)S(1)}, s32[3,64,64]{2,1,0:T(8,128)}, u32[]{:S(2)}) copy-start(s32[3,64,64]{2,1,0:T(8,128)} %param.13) | copy-start | bytes 147460
  15.5 29.3 %all-to-all-start = ((bf16[16,56,128]{2,1,0:T(8,128)(2,1)}), bf16[16,56,128]{2,1,0:T(8,128)(2,1)S(1)}, u32[]{:S(2)}, u32[]{:S(2)}) async-start(bf16[16,56,128]{2,1,0:T(8,128)(2,1)} %broadcast_in_dim.17), calls=%async_computation | async-start | bytes 458752 | tf_op jit(solution)/shard_map/all_to_all | solution.py:32
  33.1 49.4 %copy-start.3 = (bf16[192,3584]{1,0:T(8,128)(2,1)}, bf16[192,3584]{1,0:T(8,128)(2,1)S(1)}, u32[]{:S(2)}) copy-start(bf16[192,3584]{1,0:T(8,128)(2,1)S(1)} %fusion.1) | copy-start | bytes 4128772
  33.1 49.4 %collective-permute-start = (bf16[192,3584]{1,0:T(8,128)(2,1)S(1)}, bf16[192,3584]{1,0:T(8,128)(2,1)}, u32[]{:S(2)}, u32[]{:S(2)}) collective-permute-start(bf16[192,3584]{1,0:T(8,128)(2,1)S(1)} %fusion.1), channel_id=1, source_target_pairs={{0,32},{32,0},{1,33},{33,1},{2,34},{34,2},{3,35},{35,3},{4,36},{36... | collective-permute-start | bytes 4128776 | tf_op jit(solution)/shard_map/ppermute | solution.py:187
  37.0 13.8 %collective-permute-start.5 = (bf16[192,128]{1,0:T(8,128)(2,1)S(1)}, bf16[192,128]{1,0:T(8,128)(2,1)S(1)}, u32[]{:S(2)}, u32[]{:S(2)}) collective-permute-start(bf16[192,128]{1,0:T(8,128)(2,1)S(1)} %pad_convert_fusion), channel_id=1, source_target_pairs={{0,32},{32,0},{1,33},{33,1},{2,34},{34,2},{3,35},{35,3},{4,36},{36... | collective-permute-start | bytes 147464 | tf_op jit(solution)/shard_map/ppermute | solution.py:185
  44.8 8.3 %collective-permute-start.1 = (bf16[16,56,128]{2,1,0:T(8,128)(2,1)S(1)}, bf16[16,56,128]{2,1,0:T(8,128)(2,1)S(1)}, u32[]{:S(2)}, u32[]{:S(2)}) collective-permute-start(bf16[16,56,128]{2,1,0:T(8,128)(2,1)S(1)} %all-to-all-done), channel_id=1, source_target_pairs={{0,256},{256,0},{1,257},{257,1},{2,258},{258,2},{3,259},{259,3},{4... | collective-permute-start | bytes 688136 | tf_op jit(solution)/shard_map/ppermute | solution.py:165
  54.0 30.4 %collective-permute-start.2 = (bf16[1792,128]{1,0:T(8,128)(2,1)}, bf16[1792,128]{1,0:T(8,128)(2,1)}, u32[]{:S(2)}, u32[]{:S(2)}) collective-permute-start(bf16[1792,128]{1,0:T(8,128)(2,1)} %bitcast.6), channel_id=1, source_target_pairs={{0,192},{64,0},{128,64},{192,128},{1,193},{65,1},{129,65},{193,129... | collective-permute-start | bytes 1376264 | tf_op jit(solution)/shard_map/ppermute | solution.py:190
  58.4 28.3 %collective-permute-start.3 = (bf16[1792,128]{1,0:T(8,128)(2,1)}, bf16[1792,128]{1,0:T(8,128)(2,1)}, u32[]{:S(2)}, u32[]{:S(2)}) collective-permute-start(bf16[1792,128]{1,0:T(8,128)(2,1)} %bitcast.6), channel_id=1, source_target_pairs={{0,128},{64,192},{128,0},{192,64},{1,129},{65,193},{129,1},{193,65... | collective-permute-start | bytes 1376264 | tf_op jit(solution)/shard_map/ppermute | solution.py:190
  60.8 39.6 %collective-permute-start.4 = (bf16[1792,128]{1,0:T(8,128)(2,1)}, bf16[1792,128]{1,0:T(8,128)(2,1)}, u32[]{:S(2)}, u32[]{:S(2)}) collective-permute-start(bf16[1792,128]{1,0:T(8,128)(2,1)} %bitcast.6), channel_id=1, source_target_pairs={{0,64},{64,128},{128,192},{192,0},{1,65},{65,129},{129,193},{193,1... | collective-permute-start | bytes 1376264 | tf_op jit(solution)/shard_map/ppermute | solution.py:190
  70.3 22.7 %all-to-all-start.1 = ((bf16[16,32,128]{2,1,0:T(8,128)(2,1)}), bf16[16,32,128]{2,1,0:T(8,128)(2,1)S(1)}, u32[]{:S(2)}, u32[]{:S(2)}) async-start(bf16[16,32,128]{2,1,0:T(8,128)(2,1)} %broadcast_in_dim.18), calls=%async_computation.1 | async-start | bytes 262144 | tf_op jit(solution)/shard_map/all_to_all | solution.py:32
  94.2 18.2 %all-to-all-start.2 = ((bf16[8,512,128]{2,1,0:T(8,128)(2,1)}), bf16[8,512,128]{2,1,0:T(8,128)(2,1)}, u32[]{:S(2)}, u32[]{:S(2)}) async-start(bf16[8,512,128]{2,1,0:T(8,128)(2,1)} %broadcast_in_dim.20), calls=%async_computation.2 | async-start | bytes 2097152 | tf_op jit(solution)/shard_map/all_to_all | solution.py:32
  133.8 0.8 copy-start.1
  134.7 7.5 %collective-permute-start.6 = (bf16[192,896]{1,0:T(8,128)(2,1)S(1)}, bf16[192,896]{1,0:T(8,128)(2,1)S(1)}, u32[]{:S(2)}, u32[]{:S(2)}) collective-permute-start(bf16[192,896]{1,0:T(8,128)(2,1)S(1)} %slice.91), channel_id=1, source_target_pairs={{0,32},{32,0},{1,33},{33,1},{2,34},{34,2},{3,35},{35,3},{4,36},{36... | collective-permute-start | bytes 1032200 | tf_op jit(solution)/shard_map/ppermute | solution.py:204
Sparse Core Ops, SparseCore 0:
  14.9 101.1 all-gather.2

commit v3 on v2

--- a/solution.py
+++ b/solution.py
@@ -14,7 +14,7 @@
 AXES = ("yh", "x", "core", "yl", "z")
 SWAP = [(0, 1), (1, 0)]
 CHUNK = 1024
-DEPTH = 256
+DEPTH = 896
 
 
 def rms_norm(hidden_rows, norm_gain):
@@ -56,15 +56,14 @@
 
 
 def attend_kernel(
-    chunks, slots, low, high, low_weights, high_weights, context, step_keys, step_values, allowed, out, *scratch
+    chunks, slots, normed, low_weights, high_weights, context, step_keyval, allowed, own_out, other_out, *scratch
 ):
     total, query, keys, values = scratch
     step = pl.program_id(0)
     heads = query.shape[1] // HEAD_SIZE
-
-    @pl.when(step == 0)
-    def _():
-        total[...] = jnp.zeros_like(total)
+    depth = low_weights.shape[0]
+
+    def unpack():
         count, quarter = context.shape[1], HEAD_SIZE // 2
         for hi in range(context.shape[0] // 4):
             for x in range(4):
@@ -75,25 +74,42 @@
                         hi * 4 + x, :, side * quarter : (side + 1) * quarter
                     ]
 
-    @pl.when(step < chunks)
-    def _():
-        total[...] += dot(low[...], low_weights[...]) + dot(high[...], high_weights[...])
+    for chunk in range(chunks):
+
+        @pl.when(step == chunk)
+        def _():
+            low = normed[:, chunk * depth : (chunk + 1) * depth]
+            high = normed[:, (chunks + chunk) * depth : (chunks + chunk + 1) * depth]
+            both = dot(low, low_weights[...]) + dot(high, high_weights[...])
+            if chunk == 0:
+                total[...] = both
+                unpack()
+            else:
+                total[...] += both
 
     @pl.when(step == chunks - 1)
     def _():
         query[...] = total[...].astype(jnp.bfloat16)
 
-    @pl.when(step >= chunks)
-    def _():
-        rows = out.shape[0]
-        first = (step - chunks) * rows
-        for at in range(0, rows, slots):
-            here = slice(at, at + slots)
-            own = query[pl.ds(pl.multiple_of(first + at, slots), slots), :]
+    def attend_rows(first, out):
+        for at in range(0, out.shape[0], slots):
+            here = slice(first + at, first + at + slots)
+            own = query[here, :]
             own = jnp.concatenate([own[:, h * HEAD_SIZE : (h + 1) * HEAD_SIZE] for h in range(heads)], 0)
             seen = jnp.concatenate([allowed[here, :slots].astype(jnp.float32)] * heads, 0) > 0.5
-            result = attend_sample(own, keys, values, step_keys[here], step_values[here], seen, CHUNK)
-            out[here, :] = jnp.concatenate([result[h * slots : (h + 1) * slots] for h in range(heads)], 1)
+            step_keys, step_values = step_keyval[here, :HEAD_SIZE], step_keyval[here, HEAD_SIZE:]
+            result = attend_sample(own, keys, values, step_keys, step_values, seen, CHUNK)
+            out[at : at + slots, :] = jnp.concatenate(
+                [result[h * slots : (h + 1) * slots] for h in range(heads)], 1
+            )
+
+    @pl.when(step == chunks)
+    def _():
+        attend_rows(0, own_out)
+
+    @pl.when(step == chunks + 1)
+    def _():
+        attend_rows(own_out.shape[0], other_out)
 
 
 def attend(normed, query_weights, context, step_keyval, allowed, slots):
@@ -101,24 +117,20 @@
     half, cols = query_weights.shape[0], query_weights.shape[1] // 2
     tokens = context.shape[0] * context.shape[1] // 2
     chunks = half // DEPTH
-    at_once = 2 * slots
-    project_at = lambda i: jnp.minimum(i, chunks - 1)
-    attend_at = lambda i: jnp.maximum(i - chunks, 0)
+    here = pl.BlockSpec(memory_space=pltpu.VMEM)
     return pl.pallas_call(
         functools.partial(attend_kernel, chunks, slots),
-        grid=(chunks + rows // at_once,),
+        grid=(chunks + 2,),
         in_specs=[
-            pl.BlockSpec((rows, DEPTH), lambda i: (0, project_at(i))),
-            pl.BlockSpec((rows, DEPTH), lambda i: (0, chunks + project_at(i))),
-            pl.BlockSpec((DEPTH, cols), lambda i: (project_at(i), 0)),
-            pl.BlockSpec((DEPTH, cols), lambda i: (project_at(i), 1)),
-            pl.BlockSpec(context.shape, lambda i: (0, 0, 0)),
-            pl.BlockSpec((at_once, HEAD_SIZE), lambda i: (attend_at(i), 0)),
-            pl.BlockSpec((at_once, HEAD_SIZE), lambda i: (attend_at(i), 1)),
-            pl.BlockSpec((at_once, allowed.shape[1]), lambda i: (attend_at(i), 0)),
+            here,
+            pl.BlockSpec((DEPTH, cols), lambda i: (jnp.minimum(i, chunks - 1), 0)),
+            pl.BlockSpec((DEPTH, cols), lambda i: (jnp.minimum(i, chunks - 1), 1)),
+            here,
+            pl.BlockSpec(step_keyval.shape, lambda i: (0, 0)),
+            pl.BlockSpec(allowed.shape, lambda i: (0, 0)),
         ],
-        out_specs=pl.BlockSpec((at_once, cols), lambda i: (attend_at(i), 0)),
-        out_shape=jax.ShapeDtypeStruct((rows, cols), jnp.bfloat16),
+        out_specs=[here, here],
+        out_shape=[jax.ShapeDtypeStruct((rows // 2, cols), jnp.bfloat16)] * 2,
         scratch_shapes=[pltpu.VMEM((rows, cols), jnp.float32), pltpu.VMEM((rows, cols), jnp.bfloat16)]
         + [pltpu.VMEM((tokens, HEAD_SIZE), jnp.bfloat16)] * 2,
         compiler_params=pltpu.CompilerParams(vmem_limit_bytes=44 * 2**20),
@@ -127,7 +139,7 @@
             bytes_accessed=2 * features * cols,
             transcendentals=rows * tokens * cols // HEAD_SIZE,
         ),
-    )(normed, normed, query_weights, query_weights, context, step_keyval, step_keyval, allowed)
+    )(normed, query_weights, query_weights, context, step_keyval, allowed)
 
 
 def project(rows, packed):
@@ -171,6 +183,7 @@
     own_context = lax.dynamic_slice_in_dim(ctx_hidden, yh * own_tokens, own_tokens, 0)
     context = project(rms_norm(own_context, norm_gain), part_kv).astype(jnp.bfloat16)
     context = lax.all_gather(pack(context), "yl", axis=0, tiled=True)
+    part_kv = lax.optimization_barrier((part_kv, context))[0]
     context = spread(spread(context, "z").reshape(-1, 2 * quarter), ("yh", "x"))
 
     positions = lax.iota(jnp.int32, slots)
@@ -199,14 +212,14 @@
     step_keyval = dot(both_rows, kv_weights).astype(jnp.bfloat16)
     step_keyval = jnp.concatenate([step_keyval, step_keyval], 1)
     step_keyval = lax.dynamic_slice_in_dim(step_keyval, (chips - x) % chips * quarter, chips * quarter, 1)
-    attended = attend(both_rows, query_weights, context, step_keyval, allowed, slots)
-
-    mine, theirs = attended[:rows], lax.ppermute(attended[rows:], "core", SWAP)
+    mine, theirs = attend(both_rows, query_weights, context, step_keyval, allowed, slots)
+
+    theirs = lax.ppermute(theirs, "core", SWAP)
+    live_rows = (positions[None, :] < step_lengths[:, None]).reshape(rows, 1)
     first = core == 0
-    result = jnp.concatenate([jnp.where(first, mine, theirs), jnp.where(first, theirs, mine)], 1)
-    result = result.reshape(samples, slots, kv_heads * cols)
-    live_rows = positions[None, :] < step_lengths[:, None]
-    return jnp.where(live_rows[:, :, None], result, jnp.bfloat16(0.0))
+    low = jnp.where(live_rows, jnp.where(first, mine, theirs), jnp.bfloat16(0.0))
+    high = jnp.where(live_rows, jnp.where(first, theirs, mine), jnp.bfloat16(0.0))
+    return jnp.concatenate([low, high], 1).reshape(samples, slots, kv_heads * cols)
 
 
 def solution(mesh):

time: 152 us -> 150 us (0.987)
  Pallas kernels: 17.8 us -> 15.2 us
    pallas_call x1, Pallas kernels: 17.8 us -> 15.2 us  [attend(): pl.pallas_call(functools.partial(attend_kernel, chunks, slots), grid=(chu...]
    slice x2 -> x0, local copies, waits for them, and re-layouts: 2.41 us -> none  [the longest x1 2.38 us: project(): packed[:, :width]]
    slice x3 -> x4, local copies, waits for them, and re-layouts: 5.85 us -> 8.26 us  [local(): one[:, :quarter]]
    select_n x2 -> x1, other arithmetic: 2.02 us -> 0.15 us  [local(): jnp.where(live_rows, jnp.where(first, mine, theirs), jnp.bfloat16(0.0))]
  transfers between devices with their start and end apart: 11 -> 11, of which waited for: 6 -> 6; matrix products, arithmetic and copies ran while one was open for 16% -> 17% of each run, Pallas kernels for 0% -> 0%
where the time goes in v3:
time: 150 us; the launch traced here: 149 us
  starting transfers between devices  58.6 us (39%)
  waiting for transfers between devices  21.3 us (14%)
  Pallas kernels  15.2 us (10%)
  local copies, waits for them, and re-layouts  13.9 us (9%)
  between operations  13.7 us (9%)
  blocking collectives  9.96 us (7%)
  other arithmetic  9.42 us (6%)
  matrix products  6.65 us (4%)
    all_to_all x3, starting transfers between devices, spread(): lax.all_to_all(jnp.broadcast_to(block[None], (size,) + block.shape), axis...  32.5 us
    pallas_call x1, Pallas kernels, attend(): pl.pallas_call(functools.partial(attend_kernel, chunks, slots), grid=(chu...  15.2 us
    all_to_all x3, waiting for transfers between devices, spread(): lax.all_to_all(jnp.broadcast_to(block[None], (size,) + block.shape), axis...  14.6 us
    ppermute x3, starting transfers between devices, local(): lax.ppermute(part_kv, 'x', [(i, (i - turn) % chips) for i in range(chips)])  9.32 us
    slice x4, local copies, waits for them, and re-layouts, local(): one[:, :quarter]  8.26 us
    dot_general x3, matrix products, dot(): return jnp.dot(a, b, preferred_element_type=jnp.float32)  6.65 us
    ppermute x1, starting transfers between devices, local(): theirs = lax.ppermute(theirs, 'core', SWAP)  6.27 us
    all_gather x1, blocking collectives, local(): pair = lax.all_gather(jnp.concatenate([own_query, own_kv], 1), 'yl', axis=0)  6.2 us
  transfers between devices with their start and end apart: 11, of which 6 were waited for; matrix products, arithmetic and copies ran while one was open for 17% of the time, Pallas kernels for 0%

profile of v3, /device:TPU:1, one launch (start us, length us, event | category | flops | bytes accessed | tf_op | source)
XLA Modules:
  0.0 148.7 jit_solution(3651172335119156764)
XLA Ops:
  6.5 1.0 constant_dynamic-slice_fusion.1
  7.6 6.2 %all-gather = bf16[224,960]{1,0:T(8,128)(2,1)S(1)} all-gather(bf16[112,960]{1,0:T(8,128)(2,1)S(1)} %pad_maximum_fusion.4), channel_id=2, replica_groups=mesh['yh'=2,'x'=4,'core'=2,'yl'=2,'z'=16] {'yl'}, dimensions={0}, use_global_device_ids=true | all-gather | bytes 645120 | tf_op jit(solution)/shard_map/all_gather | solution.py:167
  13.9 0.1 pad_maximum_fusion.6
  13.9 0.8 pad_maximum_fusion.3
  14.8 0.7 broadcast_in_dim.21
  15.5 16.7 %all-to-all-start = ((bf16[16,56,128]{2,1,0:T(8,128)(2,1)}), bf16[16,56,128]{2,1,0:T(8,128)(2,1)S(1)}, u32[]{:S(2)}, u32[]{:S(2)}) async-start(bf16[16,56,128]{2,1,0:T(8,128)(2,1)} %broadcast_in_dim.21), calls=%async_computation | async-start | bytes 458752 | tf_op jit(solution)/shard_map/all_to_all | solution.py:32
  32.2 0.4 multiply_reduce_fusion
  32.6 0.1 rsqrt.20
  32.7 0.4 fusion.1
  33.1 3.7 %collective-permute-start = (bf16[192,3584]{1,0:T(8,128)(2,1)S(1)}, bf16[192,3584]{1,0:T(8,128)(2,1)}, u32[]{:S(2)}, u32[]{:S(2)}) collective-permute-start(bf16[192,3584]{1,0:T(8,128)(2,1)S(1)} %fusion.1), channel_id=1, source_target_pairs={{0,32},{32,0},{1,33},{33,1},{2,34},{34,2},{3,35},{35,3},{4,36},{36... | collective-permute-start | bytes 4128776 | tf_op jit(solution)/shard_map/ppermute | solution.py:200
  36.9 0.1 iota_compare_fusion.2
  37.0 1.9 %collective-permute-start.5 = (bf16[192,128]{1,0:T(8,128)(2,1)S(1)}, bf16[192,128]{1,0:T(8,128)(2,1)S(1)}, u32[]{:S(2)}, u32[]{:S(2)}) collective-permute-start(bf16[192,128]{1,0:T(8,128)(2,1)S(1)} %pad_convert_fusion), channel_id=1, source_target_pairs={{0,32},{32,0},{1,33},{33,1},{2,34},{34,2},{3,35},{35,3},{4,36},{36... | collective-permute-start | bytes 147464 | tf_op jit(solution)/shard_map/ppermute | solution.py:198
  38.9 1.1 fusion.22
  40.0 4.8 %all-to-all-done = bf16[16,56,128]{2,1,0:T(8,128)(2,1)S(1)} async-done(((bf16[16,56,128]{2,1,0:T(8,128)(2,1)}), bf16[16,56,128]{2,1,0:T(8,128)(2,1)S(1)}, u32[]{:S(2)}, u32[]{:S(2)}) %all-to-all-start) | async-done | bytes 229408 | tf_op jit(solution)/shard_map/all_to_all | solution.py:32
  44.8 4.8 %collective-permute-start.1 = (bf16[16,56,128]{2,1,0:T(8,128)(2,1)S(1)}, bf16[16,56,128]{2,1,0:T(8,128)(2,1)S(1)}, u32[]{:S(2)}, u32[]{:S(2)}) collective-permute-start(bf16[16,56,128]{2,1,0:T(8,128)(2,1)S(1)} %all-to-all-done), channel_id=1, source_target_pairs={{0,256},{256,0},{1,257},{257,1},{2,258},{258,2},{3,259},{259,3},{4... | collective-permute-start | bytes 688136 | tf_op jit(solution)/shard_map/ppermute | solution.py:177
  49.7 1.1 fusion.24
  50.8 0.6 pad_maximum_fusion.5.allowed
  51.4 1.7 %collective-permute-done.1 = bf16[16,56,128]{2,1,0:T(8,128)(2,1)S(1)} collective-permute-done((bf16[16,56,128]{2,1,0:T(8,128)(2,1)S(1)}, bf16[16,56,128]{2,1,0:T(8,128)(2,1)S(1)}, u32[]{:S(2)}, u32[]{:S(2)}) %collective-permute-start.1) | collective-permute-done | bytes 229408 | tf_op jit(solution)/shard_map/ppermute | solution.py:177
  53.2 0.8 pad_maximum_fusion.2
  54.0 1.2 fusion.26
  55.2 1.4 fusion.21
  56.6 0.1 pad_maximum_fusion.7
  56.7 3.8 %all_gather.15 = bf16[32,128]{1,0:T(8,128)(2,1)S(1)} all-gather(bf16[16,128]{1,0:T(8,128)(2,1)S(1)} %pad_maximum_fusion.7), channel_id=1, replica_groups=mesh['yh'=2,'x'=4,'core'=2,'yl'=2,'z'=16] {'yl'}, dimensions={0}, use_global_device_ids=true | all-gather | bytes 12288 | tf_op jit(solution)/shard_map/all_gather | solution.py:185
  60.4 4.4 %collective-permute-start.2 = (bf16[1792,128]{1,0:T(8,128)(2,1)}, bf16[1792,128]{1,0:T(8,128)(2,1)}, u32[]{:S(2)}, u32[]{:S(2)}) collective-permute-start(bf16[1792,128]{1,0:T(8,128)(2,1)} %bitcast.6), channel_id=1, source_target_pairs={{0,192},{64,0},{128,64},{192,128},{1,193},{65,1},{129,65},{193,129... | collective-permute-start | bytes 1376264 | tf_op jit(solution)/shard_map/ppermute | solution.py:203
  64.8 2.4 %collective-permute-start.3 = (bf16[1792,128]{1,0:T(8,128)(2,1)}, bf16[1792,128]{1,0:T(8,128)(2,1)}, u32[]{:S(2)}, u32[]{:S(2)}) collective-permute-start(bf16[1792,128]{1,0:T(8,128)(2,1)} %bitcast.6), channel_id=1, source_target_pairs={{0,128},{64,192},{128,0},{192,64},{1,129},{65,193},{129,1},{193,65... | collective-permute-start | bytes 1376264 | tf_op jit(solution)/shard_map/ppermute | solution.py:203
  67.2 2.5 %collective-permute-start.4 = (bf16[1792,128]{1,0:T(8,128)(2,1)}, bf16[1792,128]{1,0:T(8,128)(2,1)}, u32[]{:S(2)}, u32[]{:S(2)}) collective-permute-start(bf16[1792,128]{1,0:T(8,128)(2,1)} %bitcast.6), channel_id=1, source_target_pairs={{0,64},{64,128},{128,192},{192,0},{1,65},{65,129},{129,193},{193,1... | collective-permute-start | bytes 1376264 | tf_op jit(solution)/shard_map/ppermute | solution.py:203
  69.8 0.7 broadcast_in_dim.22
  70.4 9.6 %all-to-all-start.1 = ((bf16[16,32,128]{2,1,0:T(8,128)(2,1)}), bf16[16,32,128]{2,1,0:T(8,128)(2,1)S(1)}, u32[]{:S(2)}, u32[]{:S(2)}) async-start(bf16[16,32,128]{2,1,0:T(8,128)(2,1)} %broadcast_in_dim.22), calls=%async_computation.1 | async-start | bytes 262144 | tf_op jit(solution)/shard_map/all_to_all | solution.py:32
  80.1 2.4 %fusion.32 = (bf16[1792,64]{1,0:T(8,128)(2,1)}, bf16[1792,64]{1,0:T(8,128)(2,1)}) fusion(bf16[1792,128]{1,0:T(8,128)(2,1)} %bitcast.6), kind=kLoop, calls=%fused_computation.63 | loop fusion | bytes 917504 | tf_op jit(solution)/shard_map/slice | solution.py:207
  82.5 2.0 %pad_maximum_fusion.normed = bf16[384,3584]{1,0:T(8,128)(2,1)S(1)} fusion(bf16[192,3584]{1,0:T(8,128)(2,1)} %collective-permute-done, bf16[192,3584]{1,0:T(8,128)(2,1)} %copy-done.4), kind=kLoop, calls=%fused_computation | loop fusion | flops 5505024 | bytes 5505024 | tf_op jit(solution)/shard_map/concatenate | solution.py:200
  84.4 2.3 %fusion.33 = (bf16[1792,64]{1,0:T(8,128)(2,1)}, bf16[1792,64]{1,0:T(8,128)(2,1)}) fusion(bf16[1792,128]{1,0:T(8,128)(2,1)} %collective-permute-done.2), kind=kLoop, calls=%fused_computation.64 | loop fusion | bytes 917504 | tf_op jit(solution)/shard_map/slice | solution.py:207
  86.7 2.2 %fusion.34 = (bf16[1792,64]{1,0:T(8,128)(2,1)}, bf16[1792,64]{1,0:T(8,128)(2,1)}) fusion(bf16[1792,128]{1,0:T(8,128)(2,1)} %collective-permute-done.3), kind=kLoop, calls=%fused_computation.65 | loop fusion | bytes 917504 | tf_op jit(solution)/shard_map/slice | solution.py:207
  88.9 4.1 %all-to-all-done.1 = bf16[16,32,128]{2,1,0:T(8,128)(2,1)S(1)} async-done(((bf16[16,32,128]{2,1,0:T(8,128)(2,1)}), bf16[16,32,128]{2,1,0:T(8,128)(2,1)S(1)}, u32[]{:S(2)}, u32[]{:S(2)}) %all-to-all-start.1) | async-done | bytes 131104 | tf_op jit(solution)/shard_map/all_to_all | solution.py:32
  93.1 1.1 broadcast_in_dim.24
  94.2 6.2 %all-to-all-start.2 = ((bf16[8,512,128]{2,1,0:T(8,128)(2,1)}), bf16[8,512,128]{2,1,0:T(8,128)(2,1)}, u32[]{:S(2)}, u32[]{:S(2)}) async-start(bf16[8,512,128]{2,1,0:T(8,128)(2,1)} %broadcast_in_dim.24), calls=%async_computation.2 | async-start | bytes 2097152 | tf_op jit(solution)/shard_map/all_to_all | solution.py:32
  100.4 1.4 fusion.35
  101.8 4.1 %fusion.18 = bf16[384,256]{1,0:T(8,128)(2,1)S(1)} fusion(bf16[1792,64]{1,0:T(8,128)(2,1)S(1)} %get-tuple-element.28, bf16[1792,64]{1,0:T(8,128)(2,1)} %get-tuple-element.26, bf16[1792,64]{1,0:T(8,128)(2,1)} %get-tuple-element.24, bf16[1792,64]{1,0:T(8,128)(2,1)} %get-tuple-element.22, bf16[1792,64]{1,0:T(8,128)(2,1)S(1)} %get-tuple-element.27, ...), kind=kOutput, calls=%fused_computation.21 | convolution fusion | flops 724926464 | bytes 4784128 | tf_op jit(solution)/shard_map/dot_general | solution.py:27
  105.9 0.9 fusion.28.step_keyval
  106.8 5.7 %all-to-all-done.2.context = bf16[8,512,128]{2,1,0:T(8,128)(2,1)} async-done(((bf16[8,512,128]{2,1,0:T(8,128)(2,1)}), bf16[8,512,128]{2,1,0:T(8,128)(2,1)}, u32[]{:S(2)}, u32[]{:S(2)}) %all-to-all-start.2) | async-done | bytes 1048608 | tf_op jit(solution)/shard_map/all_to_all | solution.py:32
  112.4 3.6 %all-gather.3.cloned.1.call-done.low_weights.high_weights = bf16[1792,1792]{1,0:T(8,128)(2,1)} async-done(((bf16[112,1792]{1,0:T(8,128)(2,1)}), bf16[1792,1792]{1,0:T(8,128)(2,1)}) %all-gather.3.cloned.1.call-update) | async-done | bytes 6422544 | tf_op jit(solution)/shard_map/all_gather | solution.py:173
  116.0 0.9 copy-done.1
  117.0 0.9 copy-done.2
  117.8 15.2 %shard_map.73 = (bf16[192,896]{1,0:T(8,128)(2,1)S(1)}, bf16[192,896]{1,0:T(8,128)(2,1)}) custom-call(bf16[384,3584]{1,0:T(8,128)(2,1)S(1)} %pad_maximum_fusion.normed, bf16[1792,1792]{1,0:T(8,128)(2,1)} %all-gather.3.cloned.1.call-done.low_weights.high_weights, bf16[1792,1792]{1,0:T(8,128)(2,1)} %all-gather.3.cloned.1.call-done.low_weights.high_weights, ...), custom_call_target="tpu_custom_call" | custom-call | flops 5284823040 | bytes 6422528 | tf_op jit(solution)/shard_map/pallas_call | solution.py:121
  133.0 6.3 %collective-permute-start.6 = (bf16[192,896]{1,0:T(8,128)(2,1)}, bf16[192,896]{1,0:T(8,128)(2,1)S(1)}, u32[]{:S(2)}, u32[]{:S(2)}) collective-permute-start(bf16[192,896]{1,0:T(8,128)(2,1)} %get-tuple-element.18), channel_id=1, source_target_pairs={{0,32},{32,0},{1,33},{33,1},{2,34},{34,2},{3,35},{35,3},{4,36},{36... | collective-permute-start | bytes 1032200 | tf_op jit(solution)/shard_map/ppermute | solution.py:217
  139.3 0.1 lt.60
  139.4 1.4 collective-permute-done.6
  140.8 0.1 select_select_fusion.1
  140.9 0.9 pad_maximum_fusion.1
  (33 shorter events, 0.3 us)
Async XLA Ops:
  6.5 1.0 copy-start
  6.5 25.7 %copy-start.3 = (bf16[3,64,3584]{2,1,0:T(8,128)(2,1)S(1)}, bf16[3,64,3584]{2,1,0:T(8,128)(2,1)}, u32[]{:S(2)}) copy-start(bf16[3,64,3584]{2,1,0:T(8,128)(2,1)} %param.8) | copy-start | bytes 4128772
  6.5 109.5 %all-gather.3.cloned.1.call-start = ((), (), s32[]{:S(2)}) async-start(), calls=%async_computation.3 | async-start | bytes 6823936 | tf_op jit(solution)/shard_map/all_gather | solution.py:173
  7.6 25.1 %copy-start.6 = (f32[3584]{0:T(1024)S(1)}, f32[3584]{0:T(1024)}, u32[]{:S(2)}) copy-start(f32[3584]{0:T(1024)} %param.9) | copy-start | bytes 43012
  14.7 22.1 %copy-start.7 = (s32[3]{0:T(128)S(1)}, s32[3]{0:T(128)}, u32[]{:S(2)}) copy-start(s32[3]{0:T(128)} %param.12) | copy-start | bytes 40
  14.7 22.2 %copy-start.5 = (s32[3,64,64]{2,1,0:T(8,128)S(1)}, s32[3,64,64]{2,1,0:T(8,128)}, u32[]{:S(2)}) copy-start(s32[3,64,64]{2,1,0:T(8,128)} %param.13) | copy-start | bytes 147460
  15.5 29.3 %all-to-all-start = ((bf16[16,56,128]{2,1,0:T(8,128)(2,1)}), bf16[16,56,128]{2,1,0:T(8,128)(2,1)S(1)}, u32[]{:S(2)}, u32[]{:S(2)}) async-start(bf16[16,56,128]{2,1,0:T(8,128)(2,1)} %broadcast_in_dim.21), calls=%async_computation | async-start | bytes 458752 | tf_op jit(solution)/shard_map/all_to_all | solution.py:32
  33.1 49.4 %copy-start.4 = (bf16[192,3584]{1,0:T(8,128)(2,1)}, bf16[192,3584]{1,0:T(8,128)(2,1)S(1)}, u32[]{:S(2)}) copy-start(bf16[192,3584]{1,0:T(8,128)(2,1)S(1)} %fusion.1) | copy-start | bytes 4128772
  33.1 49.4 %collective-permute-start = (bf16[192,3584]{1,0:T(8,128)(2,1)S(1)}, bf16[192,3584]{1,0:T(8,128)(2,1)}, u32[]{:S(2)}, u32[]{:S(2)}) collective-permute-start(bf16[192,3584]{1,0:T(8,128)(2,1)S(1)} %fusion.1), channel_id=1, source_target_pairs={{0,32},{32,0},{1,33},{33,1},{2,34},{34,2},{3,35},{35,3},{4,36},{36... | collective-permute-start | bytes 4128776 | tf_op jit(solution)/shard_map/ppermute | solution.py:200
  37.0 13.8 %collective-permute-start.5 = (bf16[192,128]{1,0:T(8,128)(2,1)S(1)}, bf16[192,128]{1,0:T(8,128)(2,1)S(1)}, u32[]{:S(2)}, u32[]{:S(2)}) collective-permute-start(bf16[192,128]{1,0:T(8,128)(2,1)S(1)} %pad_convert_fusion), channel_id=1, source_target_pairs={{0,32},{32,0},{1,33},{33,1},{2,34},{34,2},{3,35},{35,3},{4,36},{36... | collective-permute-start | bytes 147464 | tf_op jit(solution)/shard_map/ppermute | solution.py:198
  44.8 8.3 %collective-permute-start.1 = (bf16[16,56,128]{2,1,0:T(8,128)(2,1)S(1)}, bf16[16,56,128]{2,1,0:T(8,128)(2,1)S(1)}, u32[]{:S(2)}, u32[]{:S(2)}) collective-permute-start(bf16[16,56,128]{2,1,0:T(8,128)(2,1)S(1)} %all-to-all-done), channel_id=1, source_target_pairs={{0,256},{256,0},{1,257},{257,1},{2,258},{258,2},{3,259},{259,3},{4... | collective-permute-start | bytes 688136 | tf_op jit(solution)/shard_map/ppermute | solution.py:177
  60.4 24.0 %collective-permute-start.2 = (bf16[1792,128]{1,0:T(8,128)(2,1)}, bf16[1792,128]{1,0:T(8,128)(2,1)}, u32[]{:S(2)}, u32[]{:S(2)}) collective-permute-start(bf16[1792,128]{1,0:T(8,128)(2,1)} %bitcast.6), channel_id=1, source_target_pairs={{0,192},{64,0},{128,64},{192,128},{1,193},{65,1},{129,65},{193,129... | collective-permute-start | bytes 1376264 | tf_op jit(solution)/shard_map/ppermute | solution.py:203
  64.8 21.9 %collective-permute-start.3 = (bf16[1792,128]{1,0:T(8,128)(2,1)}, bf16[1792,128]{1,0:T(8,128)(2,1)}, u32[]{:S(2)}, u32[]{:S(2)}) collective-permute-start(bf16[1792,128]{1,0:T(8,128)(2,1)} %bitcast.6), channel_id=1, source_target_pairs={{0,128},{64,192},{128,0},{192,64},{1,129},{65,193},{129,1},{193,65... | collective-permute-start | bytes 1376264 | tf_op jit(solution)/shard_map/ppermute | solution.py:203
  67.2 33.2 %collective-permute-start.4 = (bf16[1792,128]{1,0:T(8,128)(2,1)}, bf16[1792,128]{1,0:T(8,128)(2,1)}, u32[]{:S(2)}, u32[]{:S(2)}) collective-permute-start(bf16[1792,128]{1,0:T(8,128)(2,1)} %bitcast.6), channel_id=1, source_target_pairs={{0,64},{64,128},{128,192},{192,0},{1,65},{65,129},{129,193},{193,1... | collective-permute-start | bytes 1376264 | tf_op jit(solution)/shard_map/ppermute | solution.py:203
  70.4 22.6 %all-to-all-start.1 = ((bf16[16,32,128]{2,1,0:T(8,128)(2,1)}), bf16[16,32,128]{2,1,0:T(8,128)(2,1)S(1)}, u32[]{:S(2)}, u32[]{:S(2)}) async-start(bf16[16,32,128]{2,1,0:T(8,128)(2,1)} %broadcast_in_dim.22), calls=%async_computation.1 | async-start | bytes 262144 | tf_op jit(solution)/shard_map/all_to_all | solution.py:32
  94.2 18.2 %all-to-all-start.2 = ((bf16[8,512,128]{2,1,0:T(8,128)(2,1)}), bf16[8,512,128]{2,1,0:T(8,128)(2,1)}, u32[]{:S(2)}, u32[]{:S(2)}) async-start(bf16[8,512,128]{2,1,0:T(8,128)(2,1)} %broadcast_in_dim.24), calls=%async_computation.2 | async-start | bytes 2097152 | tf_op jit(solution)/shard_map/all_to_all | solution.py:32
  116.0 0.9 copy-start.1
  117.0 0.9 copy-start.2
  133.0 7.8 %collective-permute-start.6 = (bf16[192,896]{1,0:T(8,128)(2,1)}, bf16[192,896]{1,0:T(8,128)(2,1)S(1)}, u32[]{:S(2)}, u32[]{:S(2)}) collective-permute-start(bf16[192,896]{1,0:T(8,128)(2,1)} %get-tuple-element.18), channel_id=1, source_target_pairs={{0,32},{32,0},{1,33},{33,1},{2,34},{34,2},{3,35},{35,3},{4,36},{36... | collective-permute-start | bytes 1032200 | tf_op jit(solution)/shard_map/ppermute | solution.py:217
Sparse Core Ops, SparseCore 0:
  14.9 101.1 all-gather.2

commit v4 on v3

--- a/solution.py
+++ b/solution.py
@@ -133,7 +133,7 @@
         out_shape=[jax.ShapeDtypeStruct((rows // 2, cols), jnp.bfloat16)] * 2,
         scratch_shapes=[pltpu.VMEM((rows, cols), jnp.float32), pltpu.VMEM((rows, cols), jnp.bfloat16)]
         + [pltpu.VMEM((tokens, HEAD_SIZE), jnp.bfloat16)] * 2,
-        compiler_params=pltpu.CompilerParams(vmem_limit_bytes=44 * 2**20),
+        compiler_params=pltpu.CompilerParams(vmem_limit_bytes=50 * 2**20),
         cost_estimate=pl.CostEstimate(
             flops=4 * rows * cols * tokens + 2 * rows * cols * features,
             bytes_accessed=2 * features * cols,
@@ -199,9 +199,10 @@
     normed_step = rms_norm(step_hidden.reshape(rows, features), norm_gain)
     both_rows = jnp.concatenate([normed_step, lax.ppermute(normed_step, "core", SWAP)], 0)
 
-    turns = [part_kv] + [
-        lax.ppermute(part_kv, "x", [(i, (i - turn) % chips) for i in range(chips)]) for turn in range(1, chips)
-    ]
+    turned = lambda block, turn: lax.ppermute(block, "x", [(i, (i - turn) % chips) for i in range(chips)])
+    turns = [part_kv, turned(part_kv, 1)]
+    late_kv = lax.optimization_barrier((part_kv, turns[1]))[0]
+    turns += [turned(late_kv, turn) for turn in range(2, chips)]
     kv_weights = jnp.concatenate(
         [
             jnp.concatenate([one[:, :quarter] for one in turns], 1),

time: 150 us -> 146 us (0.973)
  waiting for transfers between devices: 21.3 us -> 30 us
  local copies, waits for them, and re-layouts: 13.9 us -> 8.84 us
  matrix products: 6.65 us -> 3.43 us
  starting transfers between devices: 58.6 us -> 55.7 us
    ppermute x3, waiting for transfers between devices: 0.01 us -> 10.6 us  [local(): lax.ppermute(block, 'x', [(i, (i - turn) % chips) for i in range(chips)])]
    dot_general x3, matrix products: 6.65 us -> 3.43 us  [dot(): return jnp.dot(a, b, preferred_element_type=jnp.float32)]
    slice x4, local copies, waits for them, and re-layouts: 8.26 us -> 5.05 us  [local(): one[:, :quarter]]
    unnamed x16 -> x18, local copies, waits for them, and re-layouts: 1.88 us -> 0.07 us
    all_gather x1, waiting for transfers between devices: 3.61 us -> 1.91 us  [local(): query_weights = lax.all_gather(pair_query, 'z', axis=0, tiled=True)]
  transfers between devices with their start and end apart: 11 -> 11, of which waited for: 6 -> 7; matrix products, arithmetic and copies ran while one was open for 17% -> 12% of each run, Pallas kernels for 0% -> 0%
where the time goes in v4:
time: 146 us; the launch traced here: 145 us
  starting transfers between devices  55.7 us (38%)
  waiting for transfers between devices  30 us (21%)
  Pallas kernels  15.1 us (10%)
  between operations  13.7 us (9%)
  blocking collectives  9.86 us (7%)
  local copies, waits for them, and re-layouts  8.84 us (6%)
  other arithmetic  8.51 us (6%)
  matrix products  3.43 us (2%)
    all_to_all x3, starting transfers between devices, spread(): lax.all_to_all(jnp.broadcast_to(block[None], (size,) + block.shape), axis...  31.1 us
    pallas_call x1, Pallas kernels, attend(): pl.pallas_call(functools.partial(attend_kernel, chunks, slots), grid=(chu...  15.1 us
    all_to_all x3, waiting for transfers between devices, spread(): lax.all_to_all(jnp.broadcast_to(block[None], (size,) + block.shape), axis...  14 us
    ppermute x3, waiting for transfers between devices, local(): lax.ppermute(block, 'x', [(i, (i - turn) % chips) for i in range(chips)])  10.6 us
    ppermute x3, starting transfers between devices, local(): lax.ppermute(block, 'x', [(i, (i - turn) % chips) for i in range(chips)])  9.28 us
    all_gather x1, blocking collectives, local(): pair = lax.all_gather(jnp.concatenate([own_query, own_kv], 1), 'yl', axis=0)  6.2 us
    slice x4, local copies, waits for them, and re-layouts, local(): one[:, :quarter]  5.05 us
    ppermute x1, starting transfers between devices, local(): rest_kv = lax.ppermute(half_kv, 'yh', SWAP)  4.81 us
  transfers between devices with their start and end apart: 11, of which 7 were waited for; matrix products, arithmetic and copies ran while one was open for 12% of the time, Pallas kernels for 0%

profile of v4, /device:TPU:1, one launch (start us, length us, event | category | flops | bytes accessed | tf_op | source)
XLA Modules:
  0.0 145.2 jit_solution(18370574592700194983)
XLA Ops:
  6.5 1.0 constant_dynamic-slice_fusion.1
  7.5 0.0 copy-done
  7.6 0.0 copy-start.7
  7.6 6.2 %all-gather = bf16[224,960]{1,0:T(8,128)(2,1)S(1)} all-gather(bf16[112,960]{1,0:T(8,128)(2,1)S(1)} %pad_maximum_fusion.4), channel_id=2, replica_groups=mesh['yh'=2,'x'=4,'core'=2,'yl'=2,'z'=16] {'yl'}, dimensions={0}, use_global_device_ids=true | all-gather | bytes 645120 | tf_op jit(solution)/shard_map/all_gather | solution.py:167
  13.9 0.1 pad_maximum_fusion.6
  13.9 0.8 pad_maximum_fusion.3
  14.7 0.0 all-gather.3.cloned.1.call-update
  14.8 0.7 broadcast_in_dim.21
  15.5 16.7 %all-to-all-start = ((bf16[16,56,128]{2,1,0:T(8,128)(2,1)}), bf16[16,56,128]{2,1,0:T(8,128)(2,1)S(1)}, u32[]{:S(2)}, u32[]{:S(2)}) async-start(bf16[16,56,128]{2,1,0:T(8,128)(2,1)} %broadcast_in_dim.21), calls=%async_computation | async-start | bytes 458752 | tf_op jit(solution)/shard_map/all_to_all | solution.py:32
  32.2 0.4 multiply_reduce_fusion
  32.6 0.1 rsqrt.20
  32.7 0.4 fusion.1
  33.1 3.7 %collective-permute-start = (bf16[192,3584]{1,0:T(8,128)(2,1)S(1)}, bf16[192,3584]{1,0:T(8,128)(2,1)}, u32[]{:S(2)}, u32[]{:S(2)}) collective-permute-start(bf16[192,3584]{1,0:T(8,128)(2,1)S(1)} %fusion.1), channel_id=1, source_target_pairs={{0,32},{32,0},{1,33},{33,1},{2,34},{34,2},{3,35},{35,3},{4,36},{36... | collective-permute-start | bytes 4128776 | tf_op jit(solution)/shard_map/ppermute | solution.py:200
  36.8 0.1 iota_compare_fusion.2
  37.0 1.9 %collective-permute-start.5 = (bf16[192,128]{1,0:T(8,128)(2,1)S(1)}, bf16[192,128]{1,0:T(8,128)(2,1)S(1)}, u32[]{:S(2)}, u32[]{:S(2)}) collective-permute-start(bf16[192,128]{1,0:T(8,128)(2,1)S(1)} %pad_convert_fusion), channel_id=1, source_target_pairs={{0,32},{32,0},{1,33},{33,1},{2,34},{34,2},{3,35},{35,3},{4,36},{36... | collective-permute-start | bytes 147464 | tf_op jit(solution)/shard_map/ppermute | solution.py:198
  38.9 1.1 fusion.22
  40.0 4.8 %all-to-all-done = bf16[16,56,128]{2,1,0:T(8,128)(2,1)S(1)} async-done(((bf16[16,56,128]{2,1,0:T(8,128)(2,1)}), bf16[16,56,128]{2,1,0:T(8,128)(2,1)S(1)}, u32[]{:S(2)}, u32[]{:S(2)}) %all-to-all-start) | async-done | bytes 229408 | tf_op jit(solution)/shard_map/all_to_all | solution.py:32
  44.8 4.8 %collective-permute-start.1 = (bf16[16,56,128]{2,1,0:T(8,128)(2,1)S(1)}, bf16[16,56,128]{2,1,0:T(8,128)(2,1)S(1)}, u32[]{:S(2)}, u32[]{:S(2)}) collective-permute-start(bf16[16,56,128]{2,1,0:T(8,128)(2,1)S(1)} %all-to-all-done), channel_id=1, source_target_pairs={{0,256},{256,0},{1,257},{257,1},{2,258},{258,2},{3,259},{259,3},{4... | collective-permute-start | bytes 688136 | tf_op jit(solution)/shard_map/ppermute | solution.py:177
  49.6 1.1 fusion.24
  50.8 2.4 %collective-permute-done.1 = bf16[16,56,128]{2,1,0:T(8,128)(2,1)S(1)} collective-permute-done((bf16[16,56,128]{2,1,0:T(8,128)(2,1)S(1)}, bf16[16,56,128]{2,1,0:T(8,128)(2,1)S(1)}, u32[]{:S(2)}, u32[]{:S(2)}) %collective-permute-start.1) | collective-permute-done | bytes 229408 | tf_op jit(solution)/shard_map/ppermute | solution.py:177
  53.2 0.2 fusion.26
  53.4 0.3 fusion.21
  53.8 0.1 pad_maximum_fusion.7
  53.9 3.7 %all_gather.15 = bf16[32,128]{1,0:T(8,128)(2,1)S(1)} all-gather(bf16[16,128]{1,0:T(8,128)(2,1)S(1)} %pad_maximum_fusion.7), channel_id=1, replica_groups=mesh['yh'=2,'x'=4,'core'=2,'yl'=2,'z'=16] {'yl'}, dimensions={0}, use_global_device_ids=true | all-gather | bytes 12288 | tf_op jit(solution)/shard_map/all_gather | solution.py:185
  57.5 4.4 %collective-permute-start.2 = (bf16[1792,128]{1,0:T(8,128)(2,1)S(1)}, bf16[1792,128]{1,0:T(8,128)(2,1)S(1)}, u32[]{:S(2)}, u32[]{:S(2)}) collective-permute-start(bf16[1792,128]{1,0:T(8,128)(2,1)S(1)} %bitcast.21), channel_id=1, source_target_pairs={{0,192},{64,0},{128,64},{192,128},{1,193},{65,1},{129,65},{193,129... | collective-permute-start | bytes 1376264 | tf_op jit(solution)/shard_map/ppermute | solution.py:202
  61.9 0.7 broadcast_in_dim.22
  62.6 9.7 %all-to-all-start.1 = ((bf16[16,32,128]{2,1,0:T(8,128)(2,1)}), bf16[16,32,128]{2,1,0:T(8,128)(2,1)S(1)}, u32[]{:S(2)}, u32[]{:S(2)}) async-start(bf16[16,32,128]{2,1,0:T(8,128)(2,1)} %broadcast_in_dim.22), calls=%async_computation.1 | async-start | bytes 262144 | tf_op jit(solution)/shard_map/all_to_all | solution.py:32
  72.3 1.1 fusion.32
  73.4 3.1 %pad_maximum_fusion.normed = bf16[384,3584]{1,0:T(8,128)(2,1)} fusion(bf16[192,3584]{1,0:T(8,128)(2,1)} %collective-permute-done, bf16[192,3584]{1,0:T(8,128)(2,1)S(1)} %fusion.1), kind=kLoop, calls=%fused_computation | loop fusion | flops 5505024 | bytes 5505024 | tf_op jit(solution)/shard_map/concatenate | solution.py:200
  76.6 2.4 %collective-permute-start.3 = (bf16[1792,128]{1,0:T(8,128)(2,1)S(1)}, bf16[1792,128]{1,0:T(8,128)(2,1)}, u32[]{:S(2)}, u32[]{:S(2)}) collective-permute-start(bf16[1792,128]{1,0:T(8,128)(2,1)S(1)} %bitcast.23), channel_id=1, source_target_pairs={{0,128},{64,192},{128,0},{192,64},{1,129},{65,193},{129,1},{193,65... | collective-permute-start | bytes 1376264 | tf_op jit(solution)/shard_map/ppermute | solution.py:202
  79.0 2.5 %collective-permute-start.4 = (bf16[1792,128]{1,0:T(8,128)(2,1)S(1)}, bf16[1792,128]{1,0:T(8,128)(2,1)}, u32[]{:S(2)}, u32[]{:S(2)}) collective-permute-start(bf16[1792,128]{1,0:T(8,128)(2,1)S(1)} %bitcast.24), channel_id=1, source_target_pairs={{0,64},{64,128},{128,192},{192,0},{1,65},{65,129},{129,193},{193,1... | collective-permute-start | bytes 1376264 | tf_op jit(solution)/shard_map/ppermute | solution.py:202
  81.5 1.1 fusion.33
  82.6 2.7 %all-to-all-done.1 = bf16[16,32,128]{2,1,0:T(8,128)(2,1)S(1)} async-done(((bf16[16,32,128]{2,1,0:T(8,128)(2,1)}), bf16[16,32,128]{2,1,0:T(8,128)(2,1)S(1)}, u32[]{:S(2)}, u32[]{:S(2)}) %all-to-all-start.1) | async-done | bytes 131104 | tf_op jit(solution)/shard_map/all_to_all | solution.py:32
  85.3 1.1 broadcast_in_dim.24
  86.4 4.7 %all-to-all-start.2 = ((bf16[8,512,128]{2,1,0:T(8,128)(2,1)}), bf16[8,512,128]{2,1,0:T(8,128)(2,1)S(1)}, u32[]{:S(2)}, u32[]{:S(2)}) async-start(bf16[8,512,128]{2,1,0:T(8,128)(2,1)} %broadcast_in_dim.24), calls=%async_computation.2 | async-start | bytes 2097152 | tf_op jit(solution)/shard_map/all_to_all | solution.py:32
  91.2 1.5 %fusion.34 = (bf16[1792,64]{1,0:T(8,128)(2,1)S(1)}, bf16[1792,64]{1,0:T(8,128)(2,1)S(1)}) fusion(bf16[1792,128]{1,0:T(8,128)(2,1)} %collective-permute-done.3), kind=kLoop, calls=%fused_computation.65 | loop fusion | bytes 917504 | tf_op jit(solution)/shard_map/slice | solution.py:208
  92.7 10.6 %collective-permute-done.4 = bf16[1792,128]{1,0:T(8,128)(2,1)} collective-permute-done((bf16[1792,128]{1,0:T(8,128)(2,1)S(1)}, bf16[1792,128]{1,0:T(8,128)(2,1)}, u32[]{:S(2)}, u32[]{:S(2)}) %collective-permute-start.4) | collective-permute-done | bytes 458784 | tf_op jit(solution)/shard_map/ppermute | solution.py:202
  103.2 1.3 fusion.35
  104.6 2.9 %fusion.18 = bf16[384,256]{1,0:T(8,128)(2,1)S(1)} fusion(bf16[1792,64]{1,0:T(8,128)(2,1)S(1)} %get-tuple-element.30, bf16[1792,64]{1,0:T(8,128)(2,1)S(1)} %get-tuple-element.28, bf16[1792,64]{1,0:T(8,128)(2,1)S(1)} %copy-done.5, bf16[1792,64]{1,0:T(8,128)(2,1)S(1)} %copy-done.3, bf16[1792,64]{1,0:T(8,128)(2,1)S(1)} %get-tuple-element.29, ...), kind=kOutput, calls=%fused_computation.21 | convolution fusion | flops 724926464 | bytes 4784128 | tf_op jit(solution)/shard_map/dot_general | solution.py:27
  107.5 0.2 fusion.28.step_keyval
  107.8 6.5 %all-to-all-done.2.context = bf16[8,512,128]{2,1,0:T(8,128)(2,1)S(1)} async-done(((bf16[8,512,128]{2,1,0:T(8,128)(2,1)}), bf16[8,512,128]{2,1,0:T(8,128)(2,1)S(1)}, u32[]{:S(2)}, u32[]{:S(2)}) %all-to-all-start.2) | async-done | bytes 1048608 | tf_op jit(solution)/shard_map/all_to_all | solution.py:32
  114.2 1.9 %all-gather.3.cloned.1.call-done.low_weights.high_weights = bf16[1792,1792]{1,0:T(8,128)(2,1)} async-done(((bf16[112,1792]{1,0:T(8,128)(2,1)}), bf16[1792,1792]{1,0:T(8,128)(2,1)}) %all-gather.3.cloned.1.call-update) | async-done | bytes 6422544 | tf_op jit(solution)/shard_map/all_gather | solution.py:173
  116.1 15.1 %shard_map.73 = (bf16[192,896]{1,0:T(8,128)(2,1)S(1)}, bf16[192,896]{1,0:T(8,128)(2,1)S(1)}) custom-call(bf16[384,3584]{1,0:T(8,128)(2,1)} %pad_maximum_fusion.normed, bf16[1792,1792]{1,0:T(8,128)(2,1)} %all-gather.3.cloned.1.call-done.low_weights.high_weights, bf16[1792,1792]{1,0:T(8,128)(2,1)} %all-gather.3.cloned.1.call-done.low_weights.high_weights, ...), custom_call_target="tpu_custom_call" | custom-call | flops 5284823040 | bytes 6422528 | tf_op jit(solution)/shard_map/pallas_call | solution.py:121
  131.2 4.8 %collective-permute-start.6 = (bf16[192,896]{1,0:T(8,128)(2,1)S(1)}, bf16[192,896]{1,0:T(8,128)(2,1)S(1)}, u32[]{:S(2)}, u32[]{:S(2)}) collective-permute-start(bf16[192,896]{1,0:T(8,128)(2,1)S(1)} %get-tuple-element.20), channel_id=1, source_target_pairs={{0,32},{32,0},{1,33},{33,1},{2,34},{34,2},{3,35},{35,3},{4,36},{36... | collective-permute-start | bytes 1032200 | tf_op jit(solution)/shard_map/ppermute | solution.py:218
  136.0 0.1 lt.60
  136.1 1.2 collective-permute-done.6
  137.3 0.1 select_select_fusion.1
  137.4 0.9 pad_maximum_fusion.1
  (35 shorter events, 0.3 us)
Async XLA Ops:
  6.5 1.0 copy-start
  6.5 25.7 %copy-start.1 = (bf16[3,64,3584]{2,1,0:T(8,128)(2,1)S(1)}, bf16[3,64,3584]{2,1,0:T(8,128)(2,1)}, u32[]{:S(2)}) copy-start(bf16[3,64,3584]{2,1,0:T(8,128)(2,1)} %param.8) | copy-start | bytes 4128772
  6.5 109.6 %all-gather.3.cloned.1.call-start = ((), (), s32[]{:S(2)}) async-start(), calls=%async_computation.3 | async-start | bytes 6823936 | tf_op jit(solution)/shard_map/all_gather | solution.py:173
  7.6 25.1 %copy-start.7 = (f32[3584]{0:T(1024)S(1)}, f32[3584]{0:T(1024)}, u32[]{:S(2)}) copy-start(f32[3584]{0:T(1024)} %param.9) | copy-start | bytes 43012
  14.7 22.1 %copy-start.8 = (s32[3]{0:T(128)S(1)}, s32[3]{0:T(128)}, u32[]{:S(2)}) copy-start(s32[3]{0:T(128)} %param.12) | copy-start | bytes 40
  14.7 22.2 %copy-start.6 = (s32[3,64,64]{2,1,0:T(8,128)S(1)}, s32[3,64,64]{2,1,0:T(8,128)}, u32[]{:S(2)}) copy-start(s32[3,64,64]{2,1,0:T(8,128)} %param.13) | copy-start | bytes 147460
  15.5 29.3 %all-to-all-start = ((bf16[16,56,128]{2,1,0:T(8,128)(2,1)}), bf16[16,56,128]{2,1,0:T(8,128)(2,1)S(1)}, u32[]{:S(2)}, u32[]{:S(2)}) async-start(bf16[16,56,128]{2,1,0:T(8,128)(2,1)} %broadcast_in_dim.21), calls=%async_computation | async-start | bytes 458752 | tf_op jit(solution)/shard_map/all_to_all | solution.py:32
  33.1 40.4 %collective-permute-start = (bf16[192,3584]{1,0:T(8,128)(2,1)S(1)}, bf16[192,3584]{1,0:T(8,128)(2,1)}, u32[]{:S(2)}, u32[]{:S(2)}) collective-permute-start(bf16[192,3584]{1,0:T(8,128)(2,1)S(1)} %fusion.1), channel_id=1, source_target_pairs={{0,32},{32,0},{1,33},{33,1},{2,34},{34,2},{3,35},{35,3},{4,36},{36... | collective-permute-start | bytes 4128776 | tf_op jit(solution)/shard_map/ppermute | solution.py:200
  37.0 13.8 %collective-permute-start.5 = (bf16[192,128]{1,0:T(8,128)(2,1)S(1)}, bf16[192,128]{1,0:T(8,128)(2,1)S(1)}, u32[]{:S(2)}, u32[]{:S(2)}) collective-permute-start(bf16[192,128]{1,0:T(8,128)(2,1)S(1)} %pad_convert_fusion), channel_id=1, source_target_pairs={{0,32},{32,0},{1,33},{33,1},{2,34},{34,2},{3,35},{35,3},{4,36},{36... | collective-permute-start | bytes 147464 | tf_op jit(solution)/shard_map/ppermute | solution.py:198
  44.8 8.3 %collective-permute-start.1 = (bf16[16,56,128]{2,1,0:T(8,128)(2,1)S(1)}, bf16[16,56,128]{2,1,0:T(8,128)(2,1)S(1)}, u32[]{:S(2)}, u32[]{:S(2)}) collective-permute-start(bf16[16,56,128]{2,1,0:T(8,128)(2,1)S(1)} %all-to-all-done), channel_id=1, source_target_pairs={{0,256},{256,0},{1,257},{257,1},{2,258},{258,2},{3,259},{259,3},{4... | collective-permute-start | bytes 688136 | tf_op jit(solution)/shard_map/ppermute | solution.py:177
  57.5 19.1 %collective-permute-start.2 = (bf16[1792,128]{1,0:T(8,128)(2,1)S(1)}, bf16[1792,128]{1,0:T(8,128)(2,1)S(1)}, u32[]{:S(2)}, u32[]{:S(2)}) collective-permute-start(bf16[1792,128]{1,0:T(8,128)(2,1)S(1)} %bitcast.21), channel_id=1, source_target_pairs={{0,192},{64,0},{128,64},{192,128},{1,193},{65,1},{129,65},{193,129... | collective-permute-start | bytes 1376264 | tf_op jit(solution)/shard_map/ppermute | solution.py:202
  62.6 22.8 %all-to-all-start.1 = ((bf16[16,32,128]{2,1,0:T(8,128)(2,1)}), bf16[16,32,128]{2,1,0:T(8,128)(2,1)S(1)}, u32[]{:S(2)}, u32[]{:S(2)}) async-start(bf16[16,32,128]{2,1,0:T(8,128)(2,1)} %broadcast_in_dim.22), calls=%async_computation.1 | async-start | bytes 262144 | tf_op jit(solution)/shard_map/all_to_all | solution.py:32
  76.6 14.6 %collective-permute-start.3 = (bf16[1792,128]{1,0:T(8,128)(2,1)S(1)}, bf16[1792,128]{1,0:T(8,128)(2,1)}, u32[]{:S(2)}, u32[]{:S(2)}) collective-permute-start(bf16[1792,128]{1,0:T(8,128)(2,1)S(1)} %bitcast.23), channel_id=1, source_target_pairs={{0,128},{64,192},{128,0},{192,64},{1,129},{65,193},{129,1},{193,65... | collective-permute-start | bytes 1376264 | tf_op jit(solution)/shard_map/ppermute | solution.py:202
  79.0 24.3 %collective-permute-start.4 = (bf16[1792,128]{1,0:T(8,128)(2,1)S(1)}, bf16[1792,128]{1,0:T(8,128)(2,1)}, u32[]{:S(2)}, u32[]{:S(2)}) collective-permute-start(bf16[1792,128]{1,0:T(8,128)(2,1)S(1)} %bitcast.24), channel_id=1, source_target_pairs={{0,64},{64,128},{128,192},{192,0},{1,65},{65,129},{129,193},{193,1... | collective-permute-start | bytes 1376264 | tf_op jit(solution)/shard_map/ppermute | solution.py:202
  86.4 27.8 %all-to-all-start.2 = ((bf16[8,512,128]{2,1,0:T(8,128)(2,1)}), bf16[8,512,128]{2,1,0:T(8,128)(2,1)S(1)}, u32[]{:S(2)}, u32[]{:S(2)}) async-start(bf16[8,512,128]{2,1,0:T(8,128)(2,1)} %broadcast_in_dim.24), calls=%async_computation.2 | async-start | bytes 2097152 | tf_op jit(solution)/shard_map/all_to_all | solution.py:32
  91.1 13.4 %copy-start.2 = (bf16[1792,64]{1,0:T(8,128)(2,1)S(1)}, bf16[1792,64]{1,0:T(8,128)(2,1)}, u32[]{:S(2)}) copy-start(bf16[1792,64]{1,0:T(8,128)(2,1)} %get-tuple-element.23) | copy-start | bytes 688132
  91.2 13.5 %copy-start.3 = (bf16[1792,64]{1,0:T(8,128)(2,1)S(1)}, bf16[1792,64]{1,0:T(8,128)(2,1)}, u32[]{:S(2)}) copy-start(bf16[1792,64]{1,0:T(8,128)(2,1)} %get-tuple-element.24) | copy-start | bytes 688132
  91.2 13.5 %copy-start.4 = (bf16[1792,64]{1,0:T(8,128)(2,1)S(1)}, bf16[1792,64]{1,0:T(8,128)(2,1)}, u32[]{:S(2)}) copy-start(bf16[1792,64]{1,0:T(8,128)(2,1)} %get-tuple-element.25) | copy-start | bytes 688132
  91.2 13.5 %copy-start.5 = (bf16[1792,64]{1,0:T(8,128)(2,1)S(1)}, bf16[1792,64]{1,0:T(8,128)(2,1)}, u32[]{:S(2)}) copy-start(bf16[1792,64]{1,0:T(8,128)(2,1)} %get-tuple-element.26) | copy-start | bytes 688132
  131.2 6.1 %collective-permute-start.6 = (bf16[192,896]{1,0:T(8,128)(2,1)S(1)}, bf16[192,896]{1,0:T(8,128)(2,1)S(1)}, u32[]{:S(2)}, u32[]{:S(2)}) collective-permute-start(bf16[192,896]{1,0:T(8,128)(2,1)S(1)} %get-tuple-element.20), channel_id=1, source_target_pairs={{0,32},{32,0},{1,33},{33,1},{2,34},{34,2},{3,35},{35,3},{4,36},{36... | collective-permute-start | bytes 1032200 | tf_op jit(solution)/shard_map/ppermute | solution.py:218
Sparse Core Ops, SparseCore 0:
  14.9 101.2 all-gather.2

commit v5 on v3

--- a/solution.py
+++ b/solution.py
@@ -133,7 +133,7 @@
         out_shape=[jax.ShapeDtypeStruct((rows // 2, cols), jnp.bfloat16)] * 2,
         scratch_shapes=[pltpu.VMEM((rows, cols), jnp.float32), pltpu.VMEM((rows, cols), jnp.bfloat16)]
         + [pltpu.VMEM((tokens, HEAD_SIZE), jnp.bfloat16)] * 2,
-        compiler_params=pltpu.CompilerParams(vmem_limit_bytes=44 * 2**20),
+        compiler_params=pltpu.CompilerParams(vmem_limit_bytes=50 * 2**20),
         cost_estimate=pl.CostEstimate(
             flops=4 * rows * cols * tokens + 2 * rows * cols * features,
             bytes_accessed=2 * features * cols,
@@ -199,8 +199,9 @@
     normed_step = rms_norm(step_hidden.reshape(rows, features), norm_gain)
     both_rows = jnp.concatenate([normed_step, lax.ppermute(normed_step, "core", SWAP)], 0)
 
+    late_kv = lax.optimization_barrier((part_kv, both_rows))[0]
     turns = [part_kv] + [
-        lax.ppermute(part_kv, "x", [(i, (i - turn) % chips) for i in range(chips)]) for turn in range(1, chips)
+        lax.ppermute(late_kv, "x", [(i, (i - turn) % chips) for i in range(chips)]) for turn in range(1, chips)
     ]
     kv_weights = jnp.concatenate(
         [

time: 150 us -> 146 us (0.973)
  waiting for transfers between devices: 21.3 us -> 28.3 us
  local copies, waits for them, and re-layouts: 13.9 us -> 8.99 us
  matrix products: 6.65 us -> 3.44 us
  starting transfers between devices: 58.6 us -> 57.1 us
    ppermute x3, waiting for transfers between devices: 0.01 us -> 11.6 us  [local(): lax.ppermute(late_kv, 'x', [(i, (i - turn) % chips) for i in range(chips)])]
    all_to_all x3, waiting for transfers between devices: 14.6 us -> 11.3 us  [spread(): lax.all_to_all(jnp.broadcast_to(block[None], (size,) + block.shape), axis...]
    dot_general x3, matrix products: 6.65 us -> 3.44 us  [dot(): return jnp.dot(a, b, preferred_element_type=jnp.float32)]
    slice x4, local copies, waits for them, and re-layouts: 8.26 us -> 5.21 us  [local(): one[:, :quarter]]
    unnamed x16 -> x14, local copies, waits for them, and re-layouts: 1.88 us -> 0.06 us
    all_gather x1, waiting for transfers between devices: 3.61 us -> 1.83 us  [local(): query_weights = lax.all_gather(pair_query, 'z', axis=0, tiled=True)]
    ppermute x1, starting transfers between devices: 6.27 us -> 4.74 us  [local(): theirs = lax.ppermute(theirs, 'core', SWAP)]
  transfers between devices with their start and end apart: 11 -> 11, of which waited for: 6 -> 6; matrix products, arithmetic and copies ran while one was open for 17% -> 12% of each run, Pallas kernels for 0% -> 0%
where the time goes in v5:
time: 146 us; the launch traced here: 145 us
  starting transfers between devices  57.1 us (39%)
  waiting for transfers between devices  28.3 us (19%)
  Pallas kernels  15.1 us (10%)
  between operations  13.7 us (9%)
  blocking collectives  9.86 us (7%)
  local copies, waits for them, and re-layouts  8.99 us (6%)
  other arithmetic  8.53 us (6%)
  matrix products  3.44 us (2%)
    all_to_all x3, starting transfers between devices, spread(): lax.all_to_all(jnp.broadcast_to(block[None], (size,) + block.shape), axis...  32.6 us
    pallas_call x1, Pallas kernels, attend(): pl.pallas_call(functools.partial(attend_kernel, chunks, slots), grid=(chu...  15.1 us
    ppermute x3, waiting for transfers between devices, local(): lax.ppermute(late_kv, 'x', [(i, (i - turn) % chips) for i in range(chips)])  11.6 us
    all_to_all x3, waiting for transfers between devices, spread(): lax.all_to_all(jnp.broadcast_to(block[None], (size,) + block.shape), axis...  11.3 us
    ppermute x3, starting transfers between devices, local(): lax.ppermute(late_kv, 'x', [(i, (i - turn) % chips) for i in range(chips)])  9.32 us
    all_gather x1, blocking collectives, local(): pair = lax.all_gather(jnp.concatenate([own_query, own_kv], 1), 'yl', axis=0)  6.2 us
    slice x4, local copies, waits for them, and re-layouts, local(): one[:, :quarter]  5.21 us
    ppermute x1, starting transfers between devices, local(): rest_kv = lax.ppermute(half_kv, 'yh', SWAP)  4.81 us
  transfers between devices with their start and end apart: 11, of which 6 were waited for; matrix products, arithmetic and copies ran while one was open for 12% of the time, Pallas kernels for 0%

profile of v5, /device:TPU:1, one launch (start us, length us, event | category | flops | bytes accessed | tf_op | source)
XLA Modules:
  0.0 145.0 jit_solution(5327841391707721629)
XLA Ops:
  6.5 1.0 constant_dynamic-slice_fusion.1
  7.5 0.0 copy-done
  7.6 0.0 copy-start.5
  7.6 6.2 %all-gather = bf16[224,960]{1,0:T(8,128)(2,1)S(1)} all-gather(bf16[112,960]{1,0:T(8,128)(2,1)S(1)} %pad_maximum_fusion.4), channel_id=2, replica_groups=mesh['yh'=2,'x'=4,'core'=2,'yl'=2,'z'=16] {'yl'}, dimensions={0}, use_global_device_ids=true | all-gather | bytes 645120 | tf_op jit(solution)/shard_map/all_gather | solution.py:167
  13.9 0.1 pad_maximum_fusion.6
  13.9 0.8 pad_maximum_fusion.3
  14.7 0.0 all-gather.3.cloned.1.call-update
  14.8 0.7 broadcast_in_dim.21
  15.5 16.7 %all-to-all-start = ((bf16[16,56,128]{2,1,0:T(8,128)(2,1)}), bf16[16,56,128]{2,1,0:T(8,128)(2,1)S(1)}, u32[]{:S(2)}, u32[]{:S(2)}) async-start(bf16[16,56,128]{2,1,0:T(8,128)(2,1)} %broadcast_in_dim.21), calls=%async_computation | async-start | bytes 458752 | tf_op jit(solution)/shard_map/all_to_all | solution.py:32
  32.2 0.4 multiply_reduce_fusion
  32.6 0.1 rsqrt.20
  32.7 0.4 fusion.1
  33.1 3.7 %collective-permute-start = (bf16[192,3584]{1,0:T(8,128)(2,1)S(1)}, bf16[192,3584]{1,0:T(8,128)(2,1)}, u32[]{:S(2)}, u32[]{:S(2)}) collective-permute-start(bf16[192,3584]{1,0:T(8,128)(2,1)S(1)} %fusion.1), channel_id=1, source_target_pairs={{0,32},{32,0},{1,33},{33,1},{2,34},{34,2},{3,35},{35,3},{4,36},{36... | collective-permute-start | bytes 4128776 | tf_op jit(solution)/shard_map/ppermute | solution.py:200
  36.9 0.1 iota_compare_fusion.2
  37.0 1.9 %collective-permute-start.5 = (bf16[192,128]{1,0:T(8,128)(2,1)S(1)}, bf16[192,128]{1,0:T(8,128)(2,1)S(1)}, u32[]{:S(2)}, u32[]{:S(2)}) collective-permute-start(bf16[192,128]{1,0:T(8,128)(2,1)S(1)} %pad_convert_fusion), channel_id=1, source_target_pairs={{0,32},{32,0},{1,33},{33,1},{2,34},{34,2},{3,35},{35,3},{4,36},{36... | collective-permute-start | bytes 147464 | tf_op jit(solution)/shard_map/ppermute | solution.py:198
  38.9 1.1 fusion.22
  40.0 4.8 %all-to-all-done = bf16[16,56,128]{2,1,0:T(8,128)(2,1)S(1)} async-done(((bf16[16,56,128]{2,1,0:T(8,128)(2,1)}), bf16[16,56,128]{2,1,0:T(8,128)(2,1)S(1)}, u32[]{:S(2)}, u32[]{:S(2)}) %all-to-all-start) | async-done | bytes 229408 | tf_op jit(solution)/shard_map/all_to_all | solution.py:32
  44.9 4.8 %collective-permute-start.1 = (bf16[16,56,128]{2,1,0:T(8,128)(2,1)S(1)}, bf16[16,56,128]{2,1,0:T(8,128)(2,1)S(1)}, u32[]{:S(2)}, u32[]{:S(2)}) collective-permute-start(bf16[16,56,128]{2,1,0:T(8,128)(2,1)S(1)} %all-to-all-done), channel_id=1, source_target_pairs={{0,256},{256,0},{1,257},{257,1},{2,258},{258,2},{3,259},{259,3},{4... | collective-permute-start | bytes 688136 | tf_op jit(solution)/shard_map/ppermute | solution.py:177
  49.7 1.1 fusion.24
  50.8 2.4 %collective-permute-done.1 = bf16[16,56,128]{2,1,0:T(8,128)(2,1)S(1)} collective-permute-done((bf16[16,56,128]{2,1,0:T(8,128)(2,1)S(1)}, bf16[16,56,128]{2,1,0:T(8,128)(2,1)S(1)}, u32[]{:S(2)}, u32[]{:S(2)}) %collective-permute-start.1) | collective-permute-done | bytes 229408 | tf_op jit(solution)/shard_map/ppermute | solution.py:177
  53.2 0.2 fusion.26
  53.4 0.3 fusion.21
  53.8 0.1 pad_maximum_fusion.7
  53.9 3.7 %all_gather.15 = bf16[32,128]{1,0:T(8,128)(2,1)S(1)} all-gather(bf16[16,128]{1,0:T(8,128)(2,1)S(1)} %pad_maximum_fusion.7), channel_id=1, replica_groups=mesh['yh'=2,'x'=4,'core'=2,'yl'=2,'z'=16] {'yl'}, dimensions={0}, use_global_device_ids=true | all-gather | bytes 12288 | tf_op jit(solution)/shard_map/all_gather | solution.py:185
  57.5 0.7 broadcast_in_dim.22
  58.2 9.7 %all-to-all-start.1 = ((bf16[16,32,128]{2,1,0:T(8,128)(2,1)}), bf16[16,32,128]{2,1,0:T(8,128)(2,1)S(1)}, u32[]{:S(2)}, u32[]{:S(2)}) async-start(bf16[16,32,128]{2,1,0:T(8,128)(2,1)} %broadcast_in_dim.22), calls=%async_computation.1 | async-start | bytes 262144 | tf_op jit(solution)/shard_map/all_to_all | solution.py:32
  67.9 0.0 collective-permute-done
  67.9 3.1 %pad_maximum_fusion.normed = bf16[384,3584]{1,0:T(8,128)(2,1)} fusion(bf16[192,3584]{1,0:T(8,128)(2,1)} %collective-permute-done, bf16[192,3584]{1,0:T(8,128)(2,1)S(1)} %fusion.1), kind=kLoop, calls=%fused_computation | loop fusion | flops 5505024 | bytes 5505024 | tf_op jit(solution)/shard_map/concatenate | solution.py:200
  71.1 4.4 %collective-permute-start.2 = (bf16[1792,128]{1,0:T(8,128)(2,1)S(1)}, bf16[1792,128]{1,0:T(8,128)(2,1)}, u32[]{:S(2)}, u32[]{:S(2)}) collective-permute-start(bf16[1792,128]{1,0:T(8,128)(2,1)S(1)} %bitcast.21), channel_id=1, source_target_pairs={{0,192},{64,0},{128,64},{192,128},{1,193},{65,1},{129,65},{193,129... | collective-permute-start | bytes 1376264 | tf_op jit(solution)/shard_map/ppermute | solution.py:204
  75.5 1.1 fusion.32
  76.6 2.4 %collective-permute-start.3 = (bf16[1792,128]{1,0:T(8,128)(2,1)S(1)}, bf16[1792,128]{1,0:T(8,128)(2,1)}, u32[]{:S(2)}, u32[]{:S(2)}) collective-permute-start(bf16[1792,128]{1,0:T(8,128)(2,1)S(1)} %bitcast.23), channel_id=1, source_target_pairs={{0,128},{64,192},{128,0},{192,64},{1,129},{65,193},{129,1},{193,65... | collective-permute-start | bytes 1376264 | tf_op jit(solution)/shard_map/ppermute | solution.py:204
  79.0 2.5 %collective-permute-start.4 = (bf16[1792,128]{1,0:T(8,128)(2,1)S(1)}, bf16[1792,128]{1,0:T(8,128)(2,1)}, u32[]{:S(2)}, u32[]{:S(2)}) collective-permute-start(bf16[1792,128]{1,0:T(8,128)(2,1)S(1)} %bitcast.24), channel_id=1, source_target_pairs={{0,64},{64,128},{128,192},{192,0},{1,65},{65,129},{129,193},{193,1... | collective-permute-start | bytes 1376264 | tf_op jit(solution)/shard_map/ppermute | solution.py:204
  81.5 1.1 broadcast_in_dim.24
  82.6 6.2 %all-to-all-start.2 = ((bf16[8,512,128]{2,1,0:T(8,128)(2,1)}), bf16[8,512,128]{2,1,0:T(8,128)(2,1)S(1)}, u32[]{:S(2)}, u32[]{:S(2)}) async-start(bf16[8,512,128]{2,1,0:T(8,128)(2,1)} %broadcast_in_dim.24), calls=%async_computation.2 | async-start | bytes 2097152 | tf_op jit(solution)/shard_map/all_to_all | solution.py:32
  88.9 1.4 fusion.33
  90.3 1.3 fusion.34
  91.7 11.6 %collective-permute-done.4 = bf16[1792,128]{1,0:T(8,128)(2,1)} collective-permute-done((bf16[1792,128]{1,0:T(8,128)(2,1)S(1)}, bf16[1792,128]{1,0:T(8,128)(2,1)}, u32[]{:S(2)}, u32[]{:S(2)}) %collective-permute-start.4) | collective-permute-done | bytes 458784 | tf_op jit(solution)/shard_map/ppermute | solution.py:204
  103.2 1.4 fusion.35
  104.6 2.9 %fusion.18 = bf16[384,256]{1,0:T(8,128)(2,1)S(1)} fusion(bf16[1792,64]{1,0:T(8,128)(2,1)S(1)} %get-tuple-element.30, bf16[1792,64]{1,0:T(8,128)(2,1)S(1)} %get-tuple-element.28, bf16[1792,64]{1,0:T(8,128)(2,1)S(1)} %get-tuple-element.26, bf16[1792,64]{1,0:T(8,128)(2,1)S(1)} %copy-done.3, bf16[1792,64]{1,0:T(8,128)(2,1)S(1)} %get-tuple-element.29, ...), kind=kOutput, calls=%fused_computation.21 | convolution fusion | flops 724926464 | bytes 4784128 | tf_op jit(solution)/shard_map/dot_general | solution.py:27
  107.5 0.2 fusion.28.step_keyval
  107.7 6.5 %all-to-all-done.2.context = bf16[8,512,128]{2,1,0:T(8,128)(2,1)S(1)} async-done(((bf16[8,512,128]{2,1,0:T(8,128)(2,1)}), bf16[8,512,128]{2,1,0:T(8,128)(2,1)S(1)}, u32[]{:S(2)}, u32[]{:S(2)}) %all-to-all-start.2) | async-done | bytes 1048608 | tf_op jit(solution)/shard_map/all_to_all | solution.py:32
  114.2 1.8 %all-gather.3.cloned.1.call-done.low_weights.high_weights = bf16[1792,1792]{1,0:T(8,128)(2,1)} async-done(((bf16[112,1792]{1,0:T(8,128)(2,1)}), bf16[1792,1792]{1,0:T(8,128)(2,1)}) %all-gather.3.cloned.1.call-update) | async-done | bytes 6422544 | tf_op jit(solution)/shard_map/all_gather | solution.py:173
  116.1 15.1 %shard_map.73 = (bf16[192,896]{1,0:T(8,128)(2,1)S(1)}, bf16[192,896]{1,0:T(8,128)(2,1)S(1)}) custom-call(bf16[384,3584]{1,0:T(8,128)(2,1)} %pad_maximum_fusion.normed, bf16[1792,1792]{1,0:T(8,128)(2,1)} %all-gather.3.cloned.1.call-done.low_weights.high_weights, bf16[1792,1792]{1,0:T(8,128)(2,1)} %all-gather.3.cloned.1.call-done.low_weights.high_weights, ...), custom_call_target="tpu_custom_call" | custom-call | flops 5284823040 | bytes 6422528 | tf_op jit(solution)/shard_map/pallas_call | solution.py:121
  131.1 4.7 %collective-permute-start.6 = (bf16[192,896]{1,0:T(8,128)(2,1)S(1)}, bf16[192,896]{1,0:T(8,128)(2,1)S(1)}, u32[]{:S(2)}, u32[]{:S(2)}) collective-permute-start(bf16[192,896]{1,0:T(8,128)(2,1)S(1)} %get-tuple-element.20), channel_id=1, source_target_pairs={{0,32},{32,0},{1,33},{33,1},{2,34},{34,2},{3,35},{35,3},{4,36},{36... | collective-permute-start | bytes 1032200 | tf_op jit(solution)/shard_map/ppermute | solution.py:218
  135.9 0.1 lt.60
  136.0 1.2 collective-permute-done.6
  137.1 0.1 select_select_fusion.1
  137.3 0.9 pad_maximum_fusion.1
  (31 shorter events, 0.3 us)
Async XLA Ops:
  6.5 1.0 copy-start
  6.5 25.7 %copy-start.1 = (bf16[3,64,3584]{2,1,0:T(8,128)(2,1)S(1)}, bf16[3,64,3584]{2,1,0:T(8,128)(2,1)}, u32[]{:S(2)}) copy-start(bf16[3,64,3584]{2,1,0:T(8,128)(2,1)} %param.8) | copy-start | bytes 4128772
  6.5 109.5 %all-gather.3.cloned.1.call-start = ((), (), s32[]{:S(2)}) async-start(), calls=%async_computation.3 | async-start | bytes 6823936 | tf_op jit(solution)/shard_map/all_gather | solution.py:173
  7.6 25.1 %copy-start.5 = (f32[3584]{0:T(1024)S(1)}, f32[3584]{0:T(1024)}, u32[]{:S(2)}) copy-start(f32[3584]{0:T(1024)} %param.9) | copy-start | bytes 43012
  14.7 22.1 %copy-start.6 = (s32[3]{0:T(128)S(1)}, s32[3]{0:T(128)}, u32[]{:S(2)}) copy-start(s32[3]{0:T(128)} %param.12) | copy-start | bytes 40
  14.7 22.2 %copy-start.4 = (s32[3,64,64]{2,1,0:T(8,128)S(1)}, s32[3,64,64]{2,1,0:T(8,128)}, u32[]{:S(2)}) copy-start(s32[3,64,64]{2,1,0:T(8,128)} %param.13) | copy-start | bytes 147460
  15.5 29.3 %all-to-all-start = ((bf16[16,56,128]{2,1,0:T(8,128)(2,1)}), bf16[16,56,128]{2,1,0:T(8,128)(2,1)S(1)}, u32[]{:S(2)}, u32[]{:S(2)}) async-start(bf16[16,56,128]{2,1,0:T(8,128)(2,1)} %broadcast_in_dim.21), calls=%async_computation | async-start | bytes 458752 | tf_op jit(solution)/shard_map/all_to_all | solution.py:32
  33.1 34.8 %collective-permute-start = (bf16[192,3584]{1,0:T(8,128)(2,1)S(1)}, bf16[192,3584]{1,0:T(8,128)(2,1)}, u32[]{:S(2)}, u32[]{:S(2)}) collective-permute-start(bf16[192,3584]{1,0:T(8,128)(2,1)S(1)} %fusion.1), channel_id=1, source_target_pairs={{0,32},{32,0},{1,33},{33,1},{2,34},{34,2},{3,35},{35,3},{4,36},{36... | collective-permute-start | bytes 4128776 | tf_op jit(solution)/shard_map/ppermute | solution.py:200
  37.0 13.8 %collective-permute-start.5 = (bf16[192,128]{1,0:T(8,128)(2,1)S(1)}, bf16[192,128]{1,0:T(8,128)(2,1)S(1)}, u32[]{:S(2)}, u32[]{:S(2)}) collective-permute-start(bf16[192,128]{1,0:T(8,128)(2,1)S(1)} %pad_convert_fusion), channel_id=1, source_target_pairs={{0,32},{32,0},{1,33},{33,1},{2,34},{34,2},{3,35},{35,3},{4,36},{36... | collective-permute-start | bytes 147464 | tf_op jit(solution)/shard_map/ppermute | solution.py:198
  44.9 8.3 %collective-permute-start.1 = (bf16[16,56,128]{2,1,0:T(8,128)(2,1)S(1)}, bf16[16,56,128]{2,1,0:T(8,128)(2,1)S(1)}, u32[]{:S(2)}, u32[]{:S(2)}) collective-permute-start(bf16[16,56,128]{2,1,0:T(8,128)(2,1)S(1)} %all-to-all-done), channel_id=1, source_target_pairs={{0,256},{256,0},{1,257},{257,1},{2,258},{258,2},{3,259},{259,3},{4... | collective-permute-start | bytes 688136 | tf_op jit(solution)/shard_map/ppermute | solution.py:177
  58.2 23.3 %all-to-all-start.1 = ((bf16[16,32,128]{2,1,0:T(8,128)(2,1)}), bf16[16,32,128]{2,1,0:T(8,128)(2,1)S(1)}, u32[]{:S(2)}, u32[]{:S(2)}) async-start(bf16[16,32,128]{2,1,0:T(8,128)(2,1)} %broadcast_in_dim.22), calls=%async_computation.1 | async-start | bytes 262144 | tf_op jit(solution)/shard_map/all_to_all | solution.py:32
  71.1 17.8 %collective-permute-start.2 = (bf16[1792,128]{1,0:T(8,128)(2,1)S(1)}, bf16[1792,128]{1,0:T(8,128)(2,1)}, u32[]{:S(2)}, u32[]{:S(2)}) collective-permute-start(bf16[1792,128]{1,0:T(8,128)(2,1)S(1)} %bitcast.21), channel_id=1, source_target_pairs={{0,192},{64,0},{128,64},{192,128},{1,193},{65,1},{129,65},{193,129... | collective-permute-start | bytes 1376264 | tf_op jit(solution)/shard_map/ppermute | solution.py:204
  76.6 13.7 %collective-permute-start.3 = (bf16[1792,128]{1,0:T(8,128)(2,1)S(1)}, bf16[1792,128]{1,0:T(8,128)(2,1)}, u32[]{:S(2)}, u32[]{:S(2)}) collective-permute-start(bf16[1792,128]{1,0:T(8,128)(2,1)S(1)} %bitcast.23), channel_id=1, source_target_pairs={{0,128},{64,192},{128,0},{192,64},{1,129},{65,193},{129,1},{193,65... | collective-permute-start | bytes 1376264 | tf_op jit(solution)/shard_map/ppermute | solution.py:204
  79.0 24.3 %collective-permute-start.4 = (bf16[1792,128]{1,0:T(8,128)(2,1)S(1)}, bf16[1792,128]{1,0:T(8,128)(2,1)}, u32[]{:S(2)}, u32[]{:S(2)}) collective-permute-start(bf16[1792,128]{1,0:T(8,128)(2,1)S(1)} %bitcast.24), channel_id=1, source_target_pairs={{0,64},{64,128},{128,192},{192,0},{1,65},{65,129},{129,193},{193,1... | collective-permute-start | bytes 1376264 | tf_op jit(solution)/shard_map/ppermute | solution.py:204
  82.6 31.6 %all-to-all-start.2 = ((bf16[8,512,128]{2,1,0:T(8,128)(2,1)}), bf16[8,512,128]{2,1,0:T(8,128)(2,1)S(1)}, u32[]{:S(2)}, u32[]{:S(2)}) async-start(bf16[8,512,128]{2,1,0:T(8,128)(2,1)} %broadcast_in_dim.24), calls=%async_computation.2 | async-start | bytes 2097152 | tf_op jit(solution)/shard_map/all_to_all | solution.py:32
  88.8 15.7 %copy-start.2 = (bf16[1792,64]{1,0:T(8,128)(2,1)S(1)}, bf16[1792,64]{1,0:T(8,128)(2,1)}, u32[]{:S(2)}) copy-start(bf16[1792,64]{1,0:T(8,128)(2,1)} %get-tuple-element.23) | copy-start | bytes 688132
  88.8 15.7 %copy-start.3 = (bf16[1792,64]{1,0:T(8,128)(2,1)S(1)}, bf16[1792,64]{1,0:T(8,128)(2,1)}, u32[]{:S(2)}) copy-start(bf16[1792,64]{1,0:T(8,128)(2,1)} %get-tuple-element.24) | copy-start | bytes 688132
  131.1 6.0 %collective-permute-start.6 = (bf16[192,896]{1,0:T(8,128)(2,1)S(1)}, bf16[192,896]{1,0:T(8,128)(2,1)S(1)}, u32[]{:S(2)}, u32[]{:S(2)}) collective-permute-start(bf16[192,896]{1,0:T(8,128)(2,1)S(1)} %get-tuple-element.20), channel_id=1, source_target_pairs={{0,32},{32,0},{1,33},{33,1},{2,34},{34,2},{3,35},{35,3},{4,36},{36... | collective-permute-start | bytes 1032200 | tf_op jit(solution)/shard_map/ppermute | solution.py:218
Sparse Core Ops, SparseCore 0:
  14.9 101.1 all-gather.2

commit v6 on v5

--- a/solution.py
+++ b/solution.py
@@ -52,7 +52,7 @@
         weights = jnp.exp2(scores * scale - top)
         total = total + weights.sum(-1, keepdims=True)
         attended = attended + dot(weights.astype(jnp.bfloat16), values[at : at + chunk])
-    return (attended / total).astype(jnp.bfloat16)
+    return (attended * (1.0 / total)).astype(jnp.bfloat16)
 
 
 def attend_kernel(

time: 146 us -> 146 us (level)
  no operation moved by 1% of the time
where the time goes in v6:
time: 146 us; the launch traced here: 145 us
  starting transfers between devices  57.1 us (39%)
  waiting for transfers between devices  28.3 us (19%)
  Pallas kernels  15.1 us (10%)
  between operations  13.7 us (9%)
  blocking collectives  9.86 us (7%)
  local copies, waits for them, and re-layouts  8.99 us (6%)
  other arithmetic  8.53 us (6%)
  matrix products  3.44 us (2%)
    all_to_all x3, starting transfers between devices, spread(): lax.all_to_all(jnp.broadcast_to(block[None], (size,) + block.shape), axis...  32.6 us
    pallas_call x1, Pallas kernels, attend(): pl.pallas_call(functools.partial(attend_kernel, chunks, slots), grid=(chu...  15.1 us
    ppermute x3, waiting for transfers between devices, local(): lax.ppermute(late_kv, 'x', [(i, (i - turn) % chips) for i in range(chips)])  11.6 us
    all_to_all x3, waiting for transfers between devices, spread(): lax.all_to_all(jnp.broadcast_to(block[None], (size,) + block.shape), axis...  11.3 us
    ppermute x3, starting transfers between devices, local(): lax.ppermute(late_kv, 'x', [(i, (i - turn) % chips) for i in range(chips)])  9.32 us
    all_gather x1, blocking collectives, local(): pair = lax.all_gather(jnp.concatenate([own_query, own_kv], 1), 'yl', axis=0)  6.2 us
    slice x4, local copies, waits for them, and re-layouts, local(): one[:, :quarter]  5.21 us
    ppermute x1, starting transfers between devices, local(): rest_kv = lax.ppermute(half_kv, 'yh', SWAP)  4.81 us
  transfers between devices with their start and end apart: 11, of which 6 were waited for; matrix products, arithmetic and copies ran while one was open for 12% of the time, Pallas kernels for 0%

profile of v6, /device:TPU:1, one launch (start us, length us, event | category | flops | bytes accessed | tf_op | source)
XLA Modules:
  0.0 145.0 jit_solution(5327841391707721629)
XLA Ops:
  6.5 1.0 constant_dynamic-slice_fusion.1
  7.5 0.0 copy-done
  7.6 0.0 copy-start.5
  7.6 6.2 %all-gather = bf16[224,960]{1,0:T(8,128)(2,1)S(1)} all-gather(bf16[112,960]{1,0:T(8,128)(2,1)S(1)} %pad_maximum_fusion.4), channel_id=2, replica_groups=mesh['yh'=2,'x'=4,'core'=2,'yl'=2,'z'=16] {'yl'}, dimensions={0}, use_global_device_ids=true | all-gather | bytes 645120 | tf_op jit(solution)/shard_map/all_gather | solution.py:167
  13.9 0.1 pad_maximum_fusion.6
  13.9 0.8 pad_maximum_fusion.3
  14.7 0.0 all-gather.3.cloned.1.call-update
  14.8 0.7 broadcast_in_dim.21
  15.5 16.7 %all-to-all-start = ((bf16[16,56,128]{2,1,0:T(8,128)(2,1)}), bf16[16,56,128]{2,1,0:T(8,128)(2,1)S(1)}, u32[]{:S(2)}, u32[]{:S(2)}) async-start(bf16[16,56,128]{2,1,0:T(8,128)(2,1)} %broadcast_in_dim.21), calls=%async_computation | async-start | bytes 458752 | tf_op jit(solution)/shard_map/all_to_all | solution.py:32
  32.2 0.4 multiply_reduce_fusion
  32.6 0.1 rsqrt.20
  32.7 0.4 fusion.1
  33.1 3.7 %collective-permute-start = (bf16[192,3584]{1,0:T(8,128)(2,1)S(1)}, bf16[192,3584]{1,0:T(8,128)(2,1)}, u32[]{:S(2)}, u32[]{:S(2)}) collective-permute-start(bf16[192,3584]{1,0:T(8,128)(2,1)S(1)} %fusion.1), channel_id=1, source_target_pairs={{0,32},{32,0},{1,33},{33,1},{2,34},{34,2},{3,35},{35,3},{4,36},{36... | collective-permute-start | bytes 4128776 | tf_op jit(solution)/shard_map/ppermute | solution.py:200
  36.9 0.1 iota_compare_fusion.2
  37.0 1.9 %collective-permute-start.5 = (bf16[192,128]{1,0:T(8,128)(2,1)S(1)}, bf16[192,128]{1,0:T(8,128)(2,1)S(1)}, u32[]{:S(2)}, u32[]{:S(2)}) collective-permute-start(bf16[192,128]{1,0:T(8,128)(2,1)S(1)} %pad_convert_fusion), channel_id=1, source_target_pairs={{0,32},{32,0},{1,33},{33,1},{2,34},{34,2},{3,35},{35,3},{4,36},{36... | collective-permute-start | bytes 147464 | tf_op jit(solution)/shard_map/ppermute | solution.py:198
  38.9 1.1 fusion.22
  40.0 4.8 %all-to-all-done = bf16[16,56,128]{2,1,0:T(8,128)(2,1)S(1)} async-done(((bf16[16,56,128]{2,1,0:T(8,128)(2,1)}), bf16[16,56,128]{2,1,0:T(8,128)(2,1)S(1)}, u32[]{:S(2)}, u32[]{:S(2)}) %all-to-all-start) | async-done | bytes 229408 | tf_op jit(solution)/shard_map/all_to_all | solution.py:32
  44.9 4.8 %collective-permute-start.1 = (bf16[16,56,128]{2,1,0:T(8,128)(2,1)S(1)}, bf16[16,56,128]{2,1,0:T(8,128)(2,1)S(1)}, u32[]{:S(2)}, u32[]{:S(2)}) collective-permute-start(bf16[16,56,128]{2,1,0:T(8,128)(2,1)S(1)} %all-to-all-done), channel_id=1, source_target_pairs={{0,256},{256,0},{1,257},{257,1},{2,258},{258,2},{3,259},{259,3},{4... | collective-permute-start | bytes 688136 | tf_op jit(solution)/shard_map/ppermute | solution.py:177
  49.7 1.1 fusion.24
  50.8 2.4 %collective-permute-done.1 = bf16[16,56,128]{2,1,0:T(8,128)(2,1)S(1)} collective-permute-done((bf16[16,56,128]{2,1,0:T(8,128)(2,1)S(1)}, bf16[16,56,128]{2,1,0:T(8,128)(2,1)S(1)}, u32[]{:S(2)}, u32[]{:S(2)}) %collective-permute-start.1) | collective-permute-done | bytes 229408 | tf_op jit(solution)/shard_map/ppermute | solution.py:177
  53.2 0.2 fusion.26
  53.4 0.3 fusion.21
  53.8 0.1 pad_maximum_fusion.7
  53.9 3.7 %all_gather.15 = bf16[32,128]{1,0:T(8,128)(2,1)S(1)} all-gather(bf16[16,128]{1,0:T(8,128)(2,1)S(1)} %pad_maximum_fusion.7), channel_id=1, replica_groups=mesh['yh'=2,'x'=4,'core'=2,'yl'=2,'z'=16] {'yl'}, dimensions={0}, use_global_device_ids=true | all-gather | bytes 12288 | tf_op jit(solution)/shard_map/all_gather | solution.py:185
  57.5 0.7 broadcast_in_dim.22
  58.2 9.7 %all-to-all-start.1 = ((bf16[16,32,128]{2,1,0:T(8,128)(2,1)}), bf16[16,32,128]{2,1,0:T(8,128)(2,1)S(1)}, u32[]{:S(2)}, u32[]{:S(2)}) async-start(bf16[16,32,128]{2,1,0:T(8,128)(2,1)} %broadcast_in_dim.22), calls=%async_computation.1 | async-start | bytes 262144 | tf_op jit(solution)/shard_map/all_to_all | solution.py:32
  67.9 0.0 collective-permute-done
  67.9 3.1 %pad_maximum_fusion.normed = bf16[384,3584]{1,0:T(8,128)(2,1)} fusion(bf16[192,3584]{1,0:T(8,128)(2,1)} %collective-permute-done, bf16[192,3584]{1,0:T(8,128)(2,1)S(1)} %fusion.1), kind=kLoop, calls=%fused_computation | loop fusion | flops 5505024 | bytes 5505024 | tf_op jit(solution)/shard_map/concatenate | solution.py:200
  71.1 4.4 %collective-permute-start.2 = (bf16[1792,128]{1,0:T(8,128)(2,1)S(1)}, bf16[1792,128]{1,0:T(8,128)(2,1)}, u32[]{:S(2)}, u32[]{:S(2)}) collective-permute-start(bf16[1792,128]{1,0:T(8,128)(2,1)S(1)} %bitcast.21), channel_id=1, source_target_pairs={{0,192},{64,0},{128,64},{192,128},{1,193},{65,1},{129,65},{193,129... | collective-permute-start | bytes 1376264 | tf_op jit(solution)/shard_map/ppermute | solution.py:204
  75.5 1.1 fusion.32
  76.6 2.4 %collective-permute-start.3 = (bf16[1792,128]{1,0:T(8,128)(2,1)S(1)}, bf16[1792,128]{1,0:T(8,128)(2,1)}, u32[]{:S(2)}, u32[]{:S(2)}) collective-permute-start(bf16[1792,128]{1,0:T(8,128)(2,1)S(1)} %bitcast.23), channel_id=1, source_target_pairs={{0,128},{64,192},{128,0},{192,64},{1,129},{65,193},{129,1},{193,65... | collective-permute-start | bytes 1376264 | tf_op jit(solution)/shard_map/ppermute | solution.py:204
  79.0 2.5 %collective-permute-start.4 = (bf16[1792,128]{1,0:T(8,128)(2,1)S(1)}, bf16[1792,128]{1,0:T(8,128)(2,1)}, u32[]{:S(2)}, u32[]{:S(2)}) collective-permute-start(bf16[1792,128]{1,0:T(8,128)(2,1)S(1)} %bitcast.24), channel_id=1, source_target_pairs={{0,64},{64,128},{128,192},{192,0},{1,65},{65,129},{129,193},{193,1... | collective-permute-start | bytes 1376264 | tf_op jit(solution)/shard_map/ppermute | solution.py:204
  81.5 1.1 broadcast_in_dim.24
  82.6 6.2 %all-to-all-start.2 = ((bf16[8,512,128]{2,1,0:T(8,128)(2,1)}), bf16[8,512,128]{2,1,0:T(8,128)(2,1)S(1)}, u32[]{:S(2)}, u32[]{:S(2)}) async-start(bf16[8,512,128]{2,1,0:T(8,128)(2,1)} %broadcast_in_dim.24), calls=%async_computation.2 | async-start | bytes 2097152 | tf_op jit(solution)/shard_map/all_to_all | solution.py:32
  88.9 1.4 fusion.33
  90.3 1.3 fusion.34
  91.7 11.6 %collective-permute-done.4 = bf16[1792,128]{1,0:T(8,128)(2,1)} collective-permute-done((bf16[1792,128]{1,0:T(8,128)(2,1)S(1)}, bf16[1792,128]{1,0:T(8,128)(2,1)}, u32[]{:S(2)}, u32[]{:S(2)}) %collective-permute-start.4) | collective-permute-done | bytes 458784 | tf_op jit(solution)/shard_map/ppermute | solution.py:204
  103.2 1.4 fusion.35
  104.6 2.9 %fusion.18 = bf16[384,256]{1,0:T(8,128)(2,1)S(1)} fusion(bf16[1792,64]{1,0:T(8,128)(2,1)S(1)} %get-tuple-element.30, bf16[1792,64]{1,0:T(8,128)(2,1)S(1)} %get-tuple-element.28, bf16[1792,64]{1,0:T(8,128)(2,1)S(1)} %get-tuple-element.26, bf16[1792,64]{1,0:T(8,128)(2,1)S(1)} %copy-done.3, bf16[1792,64]{1,0:T(8,128)(2,1)S(1)} %get-tuple-element.29, ...), kind=kOutput, calls=%fused_computation.21 | convolution fusion | flops 724926464 | bytes 4784128 | tf_op jit(solution)/shard_map/dot_general | solution.py:27
  107.5 0.2 fusion.28.step_keyval
  107.7 6.5 %all-to-all-done.2.context = bf16[8,512,128]{2,1,0:T(8,128)(2,1)S(1)} async-done(((bf16[8,512,128]{2,1,0:T(8,128)(2,1)}), bf16[8,512,128]{2,1,0:T(8,128)(2,1)S(1)}, u32[]{:S(2)}, u32[]{:S(2)}) %all-to-all-start.2) | async-done | bytes 1048608 | tf_op jit(solution)/shard_map/all_to_all | solution.py:32
  114.2 1.8 %all-gather.3.cloned.1.call-done.low_weights.high_weights = bf16[1792,1792]{1,0:T(8,128)(2,1)} async-done(((bf16[112,1792]{1,0:T(8,128)(2,1)}), bf16[1792,1792]{1,0:T(8,128)(2,1)}) %all-gather.3.cloned.1.call-update) | async-done | bytes 6422544 | tf_op jit(solution)/shard_map/all_gather | solution.py:173
  116.1 15.1 %shard_map.73 = (bf16[192,896]{1,0:T(8,128)(2,1)S(1)}, bf16[192,896]{1,0:T(8,128)(2,1)S(1)}) custom-call(bf16[384,3584]{1,0:T(8,128)(2,1)} %pad_maximum_fusion.normed, bf16[1792,1792]{1,0:T(8,128)(2,1)} %all-gather.3.cloned.1.call-done.low_weights.high_weights, bf16[1792,1792]{1,0:T(8,128)(2,1)} %all-gather.3.cloned.1.call-done.low_weights.high_weights, ...), custom_call_target="tpu_custom_call" | custom-call | flops 5284823040 | bytes 6422528 | tf_op jit(solution)/shard_map/pallas_call | solution.py:121
  131.1 4.7 %collective-permute-start.6 = (bf16[192,896]{1,0:T(8,128)(2,1)S(1)}, bf16[192,896]{1,0:T(8,128)(2,1)S(1)}, u32[]{:S(2)}, u32[]{:S(2)}) collective-permute-start(bf16[192,896]{1,0:T(8,128)(2,1)S(1)} %get-tuple-element.20), channel_id=1, source_target_pairs={{0,32},{32,0},{1,33},{33,1},{2,34},{34,2},{3,35},{35,3},{4,36},{36... | collective-permute-start | bytes 1032200 | tf_op jit(solution)/shard_map/ppermute | solution.py:218
  135.9 0.1 lt.60
  136.0 1.2 collective-permute-done.6
  137.1 0.1 select_select_fusion.1
  137.3 0.9 pad_maximum_fusion.1
  (31 shorter events, 0.3 us)
Async XLA Ops:
  6.5 1.0 copy-start
  6.5 25.7 %copy-start.1 = (bf16[3,64,3584]{2,1,0:T(8,128)(2,1)S(1)}, bf16[3,64,3584]{2,1,0:T(8,128)(2,1)}, u32[]{:S(2)}) copy-start(bf16[3,64,3584]{2,1,0:T(8,128)(2,1)} %param.8) | copy-start | bytes 4128772
  6.5 109.5 %all-gather.3.cloned.1.call-start = ((), (), s32[]{:S(2)}) async-start(), calls=%async_computation.3 | async-start | bytes 6823936 | tf_op jit(solution)/shard_map/all_gather | solution.py:173
  7.6 25.1 %copy-start.5 = (f32[3584]{0:T(1024)S(1)}, f32[3584]{0:T(1024)}, u32[]{:S(2)}) copy-start(f32[3584]{0:T(1024)} %param.9) | copy-start | bytes 43012
  14.7 22.1 %copy-start.6 = (s32[3]{0:T(128)S(1)}, s32[3]{0:T(128)}, u32[]{:S(2)}) copy-start(s32[3]{0:T(128)} %param.12) | copy-start | bytes 40
  14.7 22.2 %copy-start.4 = (s32[3,64,64]{2,1,0:T(8,128)S(1)}, s32[3,64,64]{2,1,0:T(8,128)}, u32[]{:S(2)}) copy-start(s32[3,64,64]{2,1,0:T(8,128)} %param.13) | copy-start | bytes 147460
  15.5 29.3 %all-to-all-start = ((bf16[16,56,128]{2,1,0:T(8,128)(2,1)}), bf16[16,56,128]{2,1,0:T(8,128)(2,1)S(1)}, u32[]{:S(2)}, u32[]{:S(2)}) async-start(bf16[16,56,128]{2,1,0:T(8,128)(2,1)} %broadcast_in_dim.21), calls=%async_computation | async-start | bytes 458752 | tf_op jit(solution)/shard_map/all_to_all | solution.py:32
  33.1 34.8 %collective-permute-start = (bf16[192,3584]{1,0:T(8,128)(2,1)S(1)}, bf16[192,3584]{1,0:T(8,128)(2,1)}, u32[]{:S(2)}, u32[]{:S(2)}) collective-permute-start(bf16[192,3584]{1,0:T(8,128)(2,1)S(1)} %fusion.1), channel_id=1, source_target_pairs={{0,32},{32,0},{1,33},{33,1},{2,34},{34,2},{3,35},{35,3},{4,36},{36... | collective-permute-start | bytes 4128776 | tf_op jit(solution)/shard_map/ppermute | solution.py:200
  37.0 13.8 %collective-permute-start.5 = (bf16[192,128]{1,0:T(8,128)(2,1)S(1)}, bf16[192,128]{1,0:T(8,128)(2,1)S(1)}, u32[]{:S(2)}, u32[]{:S(2)}) collective-permute-start(bf16[192,128]{1,0:T(8,128)(2,1)S(1)} %pad_convert_fusion), channel_id=1, source_target_pairs={{0,32},{32,0},{1,33},{33,1},{2,34},{34,2},{3,35},{35,3},{4,36},{36... | collective-permute-start | bytes 147464 | tf_op jit(solution)/shard_map/ppermute | solution.py:198
  44.9 8.3 %collective-permute-start.1 = (bf16[16,56,128]{2,1,0:T(8,128)(2,1)S(1)}, bf16[16,56,128]{2,1,0:T(8,128)(2,1)S(1)}, u32[]{:S(2)}, u32[]{:S(2)}) collective-permute-start(bf16[16,56,128]{2,1,0:T(8,128)(2,1)S(1)} %all-to-all-done), channel_id=1, source_target_pairs={{0,256},{256,0},{1,257},{257,1},{2,258},{258,2},{3,259},{259,3},{4... | collective-permute-start | bytes 688136 | tf_op jit(solution)/shard_map/ppermute | solution.py:177
  58.2 23.3 %all-to-all-start.1 = ((bf16[16,32,128]{2,1,0:T(8,128)(2,1)}), bf16[16,32,128]{2,1,0:T(8,128)(2,1)S(1)}, u32[]{:S(2)}, u32[]{:S(2)}) async-start(bf16[16,32,128]{2,1,0:T(8,128)(2,1)} %broadcast_in_dim.22), calls=%async_computation.1 | async-start | bytes 262144 | tf_op jit(solution)/shard_map/all_to_all | solution.py:32
  71.1 17.8 %collective-permute-start.2 = (bf16[1792,128]{1,0:T(8,128)(2,1)S(1)}, bf16[1792,128]{1,0:T(8,128)(2,1)}, u32[]{:S(2)}, u32[]{:S(2)}) collective-permute-start(bf16[1792,128]{1,0:T(8,128)(2,1)S(1)} %bitcast.21), channel_id=1, source_target_pairs={{0,192},{64,0},{128,64},{192,128},{1,193},{65,1},{129,65},{193,129... | collective-permute-start | bytes 1376264 | tf_op jit(solution)/shard_map/ppermute | solution.py:204
  76.6 13.7 %collective-permute-start.3 = (bf16[1792,128]{1,0:T(8,128)(2,1)S(1)}, bf16[1792,128]{1,0:T(8,128)(2,1)}, u32[]{:S(2)}, u32[]{:S(2)}) collective-permute-start(bf16[1792,128]{1,0:T(8,128)(2,1)S(1)} %bitcast.23), channel_id=1, source_target_pairs={{0,128},{64,192},{128,0},{192,64},{1,129},{65,193},{129,1},{193,65... | collective-permute-start | bytes 1376264 | tf_op jit(solution)/shard_map/ppermute | solution.py:204
  79.0 24.3 %collective-permute-start.4 = (bf16[1792,128]{1,0:T(8,128)(2,1)S(1)}, bf16[1792,128]{1,0:T(8,128)(2,1)}, u32[]{:S(2)}, u32[]{:S(2)}) collective-permute-start(bf16[1792,128]{1,0:T(8,128)(2,1)S(1)} %bitcast.24), channel_id=1, source_target_pairs={{0,64},{64,128},{128,192},{192,0},{1,65},{65,129},{129,193},{193,1... | collective-permute-start | bytes 1376264 | tf_op jit(solution)/shard_map/ppermute | solution.py:204
  82.6 31.6 %all-to-all-start.2 = ((bf16[8,512,128]{2,1,0:T(8,128)(2,1)}), bf16[8,512,128]{2,1,0:T(8,128)(2,1)S(1)}, u32[]{:S(2)}, u32[]{:S(2)}) async-start(bf16[8,512,128]{2,1,0:T(8,128)(2,1)} %broadcast_in_dim.24), calls=%async_computation.2 | async-start | bytes 2097152 | tf_op jit(solution)/shard_map/all_to_all | solution.py:32
  88.8 15.7 %copy-start.2 = (bf16[1792,64]{1,0:T(8,128)(2,1)S(1)}, bf16[1792,64]{1,0:T(8,128)(2,1)}, u32[]{:S(2)}) copy-start(bf16[1792,64]{1,0:T(8,128)(2,1)} %get-tuple-element.23) | copy-start | bytes 688132
  88.8 15.7 %copy-start.3 = (bf16[1792,64]{1,0:T(8,128)(2,1)S(1)}, bf16[1792,64]{1,0:T(8,128)(2,1)}, u32[]{:S(2)}) copy-start(bf16[1792,64]{1,0:T(8,128)(2,1)} %get-tuple-element.24) | copy-start | bytes 688132
  131.1 6.0 %collective-permute-start.6 = (bf16[192,896]{1,0:T(8,128)(2,1)S(1)}, bf16[192,896]{1,0:T(8,128)(2,1)S(1)}, u32[]{:S(2)}, u32[]{:S(2)}) collective-permute-start(bf16[192,896]{1,0:T(8,128)(2,1)S(1)} %get-tuple-element.20), channel_id=1, source_target_pairs={{0,32},{32,0},{1,33},{33,1},{2,34},{34,2},{3,35},{35,3},{4,36},{36... | collective-permute-start | bytes 1032200 | tf_op jit(solution)/shard_map/ppermute | solution.py:218
Sparse Core Ops, SparseCore 0:
  14.9 101.1 all-gather.2
